TPU v7x, 32 devices: a whole 2x2x4 slice. The times are simulated.
32 devices in a mesh: groups: 2 (over y), section: 4 (over z), head: 4 (over x, core).
Axes of the slice: x: 2, y: 2, z: 4, core: 2. Of those that a mesh axis runs over, the one named last changes fastest.
Arguments:
- queries: bfloat16 [1024, 2048], P(('groups', 'section'), 'head'), parts along dimension 0, may hold values from -16 to 16
- token_key_rows: bfloat16 [1024, 1024], P(('groups', 'section'), 'head'), parts along dimension 0, may hold values from -16 to 16
- token_value_rows: bfloat16 [1024, 1024], P(('groups', 'section'), 'head'), parts along dimension 0, may hold values from -6 to 6
- residual: bfloat16 [1024, 5376], P(('groups', 'section', 'head')), parts along dimension 0, may hold values from -6 to 6
- prefix: int32 [8], P('groups'), parts along dimension 0, may hold values from 0 to 128, as said below
- out_weight: bfloat16 [2048, 5376], P('head', 'section'), may hold values from -1 to 1
- post_gain: float32 [5376], replicated, may hold values from 0.25 to 1.75
Outputs:
- layer_out: bfloat16 [1024, 5376], P(('groups', 'section', 'head')), parts along dimension 0
There are 2 independent parts, one for each index of `groups`. A program takes and returns all parts, laid end to end along the dimension named above; an argument that names none is the same for every part. Nothing has to cross between parts.
Inputs may be any that keep to these rules, and one draw needn't show every extreme that they name: `prefix`: some section at index 1 or higher has the most, 128.
All inputs are finite; a program needn't handle non-finite values.
Results may differ from a plain program's by a relative error of at most 0.012.
Values may be sent and summed in bfloat16 or wider, within the bound.
No kernel may reach another device: no remote copies, remote signals or barrier semaphores. Data moves between devices by JAX's collectives and lax.ppermute only.
A program may use at most 64 MiB of HBM per device.

v0:
```python
import functools

import jax
import jax.numpy as jnp
from jax import lax
from jax.experimental import pallas as pl
from jax.experimental.pallas import tpu as pltpu
from jax.sharding import PartitionSpec as P

HEAD_SIZE = 128


score_scale = 168.0 ** (-0.5)
floor_value = -1e30
norm_eps = 1e-06
vmem_bytes = 24 * 2**20
owner_flips = ((3, 1), (2, 0))
most_paired = 8

in_vmem = pl.BlockSpec(memory_space=pltpu.VMEM)
in_smem = pl.BlockSpec(memory_space=pltpu.SMEM)
in_hbm = pl.BlockSpec(memory_space=pltpu.HBM)
anywhere = pl.BlockSpec(memory_space=pl.ANY)


no_cost = pl.CostEstimate(flops=0, transcendentals=0, bytes_accessed=0)
project_cost = pl.CostEstimate(flops=3 * 10**9, transcendentals=0, bytes_accessed=0)


def is_power(count):
    return count & (count - 1) == 0


def rotated(value, axis, steps):
    count = lax.axis_size(axis)
    return lax.ppermute(value, axis, [(at, (at + steps) % count) for at in range(count)])


def exchanged(value, axis, flip):
    count = lax.axis_size(axis)
    return lax.ppermute(value, axis, [(at, at ^ flip) for at in range(count)])


def crossed(value, flip):
    sections, heads = lax.axis_size("section"), lax.axis_size("head")
    pairs = [
        (section * heads + head, (section ^ flip) * heads + (head ^ 1))
        for section in range(sections)
        for head in range(heads)
    ]
    return lax.ppermute(value, ("section", "head"), pairs)


def earlier_sections(own_rows, reach):
    held = own_rows[None]
    stride = 1
    while stride <= reach:
        moved_count = min(stride, reach + 1 - stride)
        held = jnp.concatenate([held, rotated(held[:moved_count], "section", stride)], axis=0)
        stride = stride * 2
    return held[:0:-1].reshape(reach * own_rows.shape[0], own_rows.shape[1])


def head_columns(head):
    return slice(head * HEAD_SIZE, (head + 1) * HEAD_SIZE)


def stacked_queries(query_ref, key_head, group_width):
    first = key_head * group_width
    return jnp.concatenate(
        [query_ref[:, head_columns(head)] for head in range(first, first + group_width)], axis=0
    )


def scaled_scores(queries, keys):
    product = lax.dot_general(
        queries, keys, (((1,), (1,)), ((), ())), preferred_element_type=jnp.float32
    )
    return product * score_scale


def own_kernel(
    prefix_in,
    query_in,
    key_in,
    value_in,
    weight_in,
    query_ref,
    value_ref,
    weight_ref,
    score_ref,
    bias_ref,
    key_ref,
    prefix_ref,
    sems,
):
    loads = [
        pltpu.make_async_copy(source, target, sems.at[at])
        for at, (source, target) in enumerate(
            (
                (prefix_in, prefix_ref),
                (query_in, query_ref),
                (key_in, key_ref),
                (value_in, value_ref),
                (weight_in, weight_ref),
            )
        )
    ]
    for load in loads:
        load.start()
    row_count = query_ref.shape[0]
    key_heads = key_ref.shape[1] // HEAD_SIZE
    group_width = query_ref.shape[1] // (key_heads * HEAD_SIZE)
    shape = (row_count, row_count)
    visible = lax.broadcasted_iota(jnp.int32, shape, 1) <= lax.broadcasted_iota(jnp.int32, shape, 0)
    visible = jnp.concatenate([visible] * group_width, axis=0)
    for load in loads[:3]:
        load.wait()
    section_index = lax.axis_index("section")
    seen_tokens = jnp.minimum(section_index * row_count, prefix_ref[section_index])
    old_pos = lax.broadcasted_iota(jnp.int32, bias_ref.shape, 1) - bias_ref.shape[1]
    bias_ref[...] = jnp.where(old_pos >= -seen_tokens, 0.0, floor_value)
    for key_head in range(key_heads):
        queries = stacked_queries(query_ref, key_head, group_width)
        scores = scaled_scores(queries, key_ref[:, head_columns(key_head)])
        score_ref[key_head] = jnp.where(visible, scores, floor_value)
    for load in loads[3:]:
        load.wait()


def weigh_kernel(query_ref, score_ref, bias_ref, old_key_ref, prob_ref, scale_ref):
    row_count = query_ref.shape[0]
    group_width = score_ref.shape[1] // row_count
    bias = jnp.concatenate([bias_ref[...]] * group_width, axis=0)
    for key_head in range(score_ref.shape[0]):
        queries = stacked_queries(query_ref, key_head, group_width)
        old_scores = scaled_scores(queries, old_key_ref[:, head_columns(key_head)]) + bias
        masked = jnp.concatenate([old_scores, score_ref[key_head]], axis=1)
        row_max = jnp.max(masked, axis=-1, keepdims=True)
        probs = jnp.exp(masked - row_max)
        denominator = jnp.sum(probs, axis=-1, keepdims=True)
        prob_ref[key_head] = probs.astype(jnp.bfloat16)
        scale_ref[key_head] = jnp.broadcast_to(1.0 / denominator, scale_ref.shape[1:])


def combine_kernel(prob_ref, scale_ref, value_ref, old_value_ref, *out_refs):
    whole_ref = out_refs[-1]
    row_count = whole_ref.shape[0]
    group_width = prob_ref.shape[1] // row_count
    for key_head in range(prob_ref.shape[0]):
        columns = head_columns(key_head)
        values = jnp.concatenate([old_value_ref[:, columns], value_ref[:, columns]], axis=0)
        combined = jnp.dot(prob_ref[key_head], values, preferred_element_type=jnp.float32)
        combined = (combined * scale_ref[key_head]).astype(jnp.bfloat16)
        for member in range(group_width):
            rows = slice(member * row_count, (member + 1) * row_count)
            whole_ref[:, head_columns(key_head * group_width + member)] = combined[rows]
    if len(out_refs) > 1:
        head_index = lax.axis_index("head")
        for out_ref, flips in zip(out_refs[:2], owner_flips, strict=True):
            own_rows = out_ref.shape[0] // len(flips)
            for at, flip in enumerate(flips):
                first = pl.multiple_of((head_index ^ flip) * own_rows, own_rows)
                out_ref[at * own_rows : (at + 1) * own_rows] = whole_ref[pl.ds(first, own_rows), :]


def attend(queries, keys, values, prefix, turned_weight, reach, in_halves):
    row_count = queries.shape[0]
    key_heads = keys.shape[1] // HEAD_SIZE
    stacked_rows = queries.shape[1] // (key_heads * HEAD_SIZE) * row_count
    params = pltpu.CompilerParams(vmem_limit_bytes=vmem_bytes)
    old_keys = earlier_sections(keys, reach)
    old_values = earlier_sections(values, reach)
    like = lambda array: jax.ShapeDtypeStruct(array.shape, array.dtype)
    own_queries, own_values, weight, scores, bias = pl.pallas_call(
        own_kernel,
        out_shape=(
            like(queries),
            like(values),
            like(turned_weight),
            jax.ShapeDtypeStruct((key_heads, stacked_rows, row_count), jnp.float32),
            jax.ShapeDtypeStruct((row_count, reach * row_count), jnp.float32),
        ),
        in_specs=[in_hbm] * 5,
        out_specs=(in_vmem,) * 5,
        scratch_shapes=[
            pltpu.VMEM(keys.shape, keys.dtype),
            pltpu.SMEM(prefix.shape, prefix.dtype),
            pltpu.SemaphoreType.DMA((5,)),
        ],
        compiler_params=params,
        cost_estimate=no_cost,
        name="own_scores",
    )(*(pltpu.with_memory_space_constraint(array, pltpu.HBM) for array in (prefix, queries, keys, values, turned_weight)))
    half = jax.ShapeDtypeStruct((row_count // 2, queries.shape[1]), queries.dtype)
    probs, scales = pl.pallas_call(
        weigh_kernel,
        out_shape=(
            jax.ShapeDtypeStruct(
                (key_heads, stacked_rows, (reach + 1) * row_count), jnp.bfloat16
            ),
            jax.ShapeDtypeStruct((key_heads, stacked_rows, HEAD_SIZE), jnp.float32),
        ),
        in_specs=[in_vmem] * 4,
        out_specs=(in_vmem,) * 2,
        compiler_params=params,
        cost_estimate=no_cost,
        name="weigh",
    )(own_queries, scores, bias, old_keys)
    attention = pl.pallas_call(
        combine_kernel,
        out_shape=(half, half) if in_halves else like(queries),
        in_specs=[in_vmem] * 4,
        out_specs=(in_vmem, in_vmem) if in_halves else in_vmem,
        scratch_shapes=[pltpu.VMEM(queries.shape, queries.dtype)] if in_halves else [],
        compiler_params=params,
        cost_estimate=no_cost,
        name="attend",
    )(probs, scales, own_values, old_values)
    return attention, weight


def project_kernel(counts, *refs):
    chunks = []
    for count in counts:
        chunk, refs = refs[:count], refs[count:]
        chunks.append(chunk if count == 2 else [chunk[0].at[0], chunk[0].at[1]])
    weight_refs, sent_ref, kept_ref = refs[:2], *refs[-2:]
    product = sum(
        lax.dot_general(
            jnp.concatenate([chunk[at][...] for chunk in chunks], axis=0),
            weight_ref[...],
            (((1,), (1,)), ((), ())),
            preferred_element_type=jnp.float32,
        )
        for at, weight_ref in enumerate(weight_refs)
    )
    rows = sent_ref.shape[1]
    for at in range(len(chunks)):
        first = 2 * rows * at
        sent_ref[at] = product[first : first + rows].astype(jnp.bfloat16)
        kept_ref[at] = product[first + rows : first + 2 * rows]


def project(chunks, weights, earlier):
    shape = (len(chunks), chunks[0][0].shape[-2] // 2, weights[0].shape[0])
    given = [array for chunk in chunks for array in chunk] + list(weights)
    return pl.pallas_call(
        functools.partial(project_kernel, [len(chunk) for chunk in chunks]),
        out_shape=(
            jax.ShapeDtypeStruct(shape, jnp.bfloat16),
            jax.ShapeDtypeStruct(shape, jnp.float32),
        ),
        in_specs=[in_vmem] * len(given) + [anywhere] * len(earlier),
        out_specs=(in_vmem, in_vmem),
        compiler_params=pltpu.CompilerParams(vmem_limit_bytes=vmem_bytes),
        cost_estimate=project_cost,
        name="project",
    )(*given, *earlier)


def stack_kernel(own_ref, other_ref, _, out_ref):
    out_ref[0] = own_ref[...]
    out_ref[1] = other_ref[...]


def stacked_after(own, other, earlier):
    return pl.pallas_call(
        stack_kernel,
        out_shape=jax.ShapeDtypeStruct((2, *own.shape), own.dtype),
        in_specs=[in_vmem, in_vmem, anywhere],
        out_specs=in_vmem,
        compiler_params=pltpu.CompilerParams(vmem_limit_bytes=vmem_bytes),
        cost_estimate=no_cost,
        name="stack",
    )(own, other, earlier)


def finish_kernel(half_ref, arrived_ref, _, out_ref):
    out_ref[...] = (half_ref[...] + arrived_ref[...].astype(jnp.float32)).astype(out_ref.dtype)


def finish_after(half, arrived, earlier):
    return pl.pallas_call(
        finish_kernel,
        out_shape=jax.ShapeDtypeStruct(half.shape, jnp.bfloat16),
        in_specs=[in_vmem, in_vmem, anywhere],
        out_specs=in_vmem,
        compiler_params=pltpu.CompilerParams(vmem_limit_bytes=vmem_bytes),
        cost_estimate=no_cost,
        name="finish",
    )(half, arrived, earlier)


def squares_kernel(has_earlier, *refs):
    *piece_refs, out_ref = refs
    total = piece_refs.pop()[:, :1] if has_earlier else 0.0
    for piece_ref in piece_refs:
        piece = piece_ref[...].astype(jnp.float32)
        total = total + jnp.sum(piece * piece, axis=-1, keepdims=True)
    out_ref[...] = jnp.broadcast_to(total, out_ref.shape)


def squares(pieces, earlier):
    given = list(pieces) if earlier is None else [*pieces, earlier]
    return pl.pallas_call(
        functools.partial(squares_kernel, earlier is not None),
        out_shape=jax.ShapeDtypeStruct((pieces[0].shape[0], HEAD_SIZE), jnp.float32),
        in_specs=[in_vmem] * len(given),
        out_specs=in_vmem,
        compiler_params=pltpu.CompilerParams(vmem_limit_bytes=vmem_bytes),
        cost_estimate=no_cost,
        name="squares",
    )(*given)


def norm_kernel(count, *refs):
    piece_refs = refs[:count]
    squares_ref, residual_ref, gain_ref, out_ref, piece_ref = refs[count:]
    width = piece_ref.shape[2]
    for at, moved_ref in enumerate(piece_refs):
        piece_ref[at] = moved_ref[...].astype(jnp.float32)
    last = piece_ref[last_flip(count)]
    square = squares_ref[:, :1] + jnp.sum(last * last, axis=-1, keepdims=True)
    scale = lax.rsqrt(square / (count * width) + norm_eps)
    section_index = lax.axis_index("section")
    for at in range(count):
        place = slice(at * width, (at + 1) * width)
        normed = piece_ref[section_index ^ at] * scale * gain_ref[:, place]
        out_ref[:, place] = (residual_ref[:, place].astype(jnp.float32) + normed).astype(jnp.bfloat16)


def last_flip(section_total):
    return section_flips(section_total)[-1][-1]


def section_flips(section_total):
    return [[0], list(range(1, section_total - 1)), [section_total - 1]]


def norm(pieces, residual, post_gain):
    early = None
    for group in section_flips(len(pieces))[:-1]:
        early = squares([pieces[flip] for flip in group], early)
    return pl.pallas_call(
        functools.partial(norm_kernel, len(pieces)),
        out_shape=jax.ShapeDtypeStruct(residual.shape, jnp.bfloat16),
        in_specs=[in_vmem] * (len(pieces) + 3),
        out_specs=in_vmem,
        scratch_shapes=[pltpu.VMEM((len(pieces), *pieces[0].shape), jnp.float32)],
        compiler_params=pltpu.CompilerParams(vmem_limit_bytes=vmem_bytes),
        cost_estimate=no_cost,
        name="norm",
    )(*pieces, early, residual, post_gain[None, :])


def local(queries, token_key_rows, token_value_rows, residual, prefix, out_weight, post_gain):
    own_rows = residual.shape[0]
    section_total = lax.axis_size("section")
    head_total = lax.axis_size("head")
    reach = 3 * section_total // 8
    in_halves = (
        2 < section_total <= most_paired and is_power(section_total) and head_total == 4
    )
    turned = out_weight.T
    attention, turned_weight = attend(
        queries, token_key_rows, token_value_rows, prefix, turned, reach, in_halves
    )
    if in_halves:
        weights = [turned_weight, exchanged(turned, "head", 1)]
        sent, kept = attention
        whole = jnp.stack([kept, exchanged(sent, "head", 1)])
        gathered = {0: [whole], 1: [exchanged(whole, "section", 1)]}
        for flip in range(2, section_total):
            if is_power(flip):
                gathered[flip] = [exchanged(kept, "section", flip), crossed(sent, flip)]
        sent, halves, arrivals = None, [], []
        groups = section_flips(section_total)
        for group in groups:
            for flip in group:
                if flip not in gathered:
                    lowest = flip & -flip
                    [source] = gathered[flip ^ lowest]
                    gathered[flip] = [exchanged(source, "section", lowest)]
            chunks = [gathered[flip] for flip in group]
            sent, half = project(chunks, weights, [] if sent is None else [sent])
            halves.append(half)
            arrivals.append(exchanged(sent, "head", 2))
            if group is groups[0]:
                for flip in range(2, section_total):
                    if is_power(flip):
                        gathered[flip] = [stacked_after(*gathered[flip], sent)]
        ready = {
            flip: (half[at], arrived[at])
            for group, half, arrived in zip(groups, halves, arrivals, strict=True)
            for at, flip in enumerate(group)
        }
        totals = {
            flip: half + arrived.astype(jnp.float32)
            for flip, (half, arrived) in ready.items()
            if flip != 1
        }
        sends = {flip: totals[flip].astype(jnp.bfloat16) for flip in range(2, section_total)}
        sends[1] = finish_after(*ready[1], sends[2])
        pieces = [totals[0]] + [
            exchanged(sends[flip], "section", flip) for flip in range(1, section_total)
        ]
        return norm(pieces, residual, post_gain)
    gathered = lax.all_gather(attention, "section", axis=0, tiled=True)
    product = jnp.dot(gathered, turned_weight.T, preferred_element_type=jnp.float32)
    product = product.astype(jnp.bfloat16).reshape(-1, head_total, own_rows, product.shape[-1])
    sums = lax.psum_scatter(product, "head", scatter_dimension=1, tiled=False)
    pieces = lax.all_to_all(sums, "section", 0, 0)
    summed = jnp.transpose(pieces, (1, 0, 2)).reshape(own_rows, -1).astype(jnp.float32)
    mean_square = jnp.mean(summed * summed, axis=-1, keepdims=True)
    normed = summed * lax.rsqrt(mean_square + norm_eps) * post_gain[None, :]
    return (residual.astype(jnp.float32) + normed).astype(jnp.bfloat16)


def solution(mesh):
    placed = (
        P(("groups", "section"), "head"),
        P(("groups", "section"), "head"),
        P(("groups", "section"), "head"),
        P(("groups", "section", "head"), None),
        P("groups"),
        P("head", "section"),
        P(),
    )
    return jax.shard_map(
        local,
        mesh=mesh,
        in_specs=placed,
        out_specs=P(("groups", "section", "head"), None),
        check_vma=False,
    )
```

profile of v0, /device:TPU:0, one launch (start us, length us, event | category | flops | bytes accessed | tf_op | source)
XLA Modules:
  0.0 37.6 jit_solution(11820485364594340882)
XLA Ops:
  0.0 0.5 %collective-permute-start.3 = (bf16[1344,512]{1,0:T(8,128)(2,1)}, bf16[1344,512]{1,0:T(8,128)(2,1)S(1)}, u32[]{:S(2)}, u32[]{:S(2)}) collective-permute-start(bf16[1344,512]{1,0:T(8,128)(2,1)} %bitcast.20), channel_id=1, source_target_pairs={{0,1},{1,0},{2,3},{3,2},{4,5},{5,4},{6,7},{7,6},{8,9},{9,8},{10,11... | collective-permute-start | bytes 4128776 | tf_op jit(solution)/shard_map/ppermute | solution.py:41
  0.5 2.6 %collective-permute-start = (bf16[1,128,256]{2,1,0:T(8,128)(2,1)}, bf16[1,128,256]{2,1,0:T(8,128)(2,1)S(1)}, u32[]{:S(2)}, u32[]{:S(2)}) collective-permute-start(bf16[1,128,256]{2,1,0:T(8,128)(2,1)} %bitcast.22), channel_id=1, source_target_pairs={{0,4},{4,8},{8,12},{12,0},{1,5},{5,9},{9,13},{13,1},{2,6},{6,10},{... | collective-permute-start | bytes 196616 | tf_op jit(solution)/shard_map/ppermute | solution.py:36
  3.0 0.0 copy-start.1
  3.0 1.6 %collective-permute-start.1 = (bf16[1,128,256]{2,1,0:T(8,128)(2,1)}, bf16[1,128,256]{2,1,0:T(8,128)(2,1)S(1)}, u32[]{:S(2)}, u32[]{:S(2)}) collective-permute-start(bf16[1,128,256]{2,1,0:T(8,128)(2,1)} %bitcast.23), channel_id=1, source_target_pairs={{0,4},{4,8},{8,12},{12,0},{1,5},{5,9},{9,13},{13,1},{2,6},{6,10},{... | collective-permute-start | bytes 196616 | tf_op jit(solution)/shard_map/ppermute | solution.py:36
  4.6 1.5 %own_scores.1 = (bf16[128,512]{1,0:T(8,128)(2,1)S(1)}, bf16[128,256]{1,0:T(8,128)(2,1)S(1)}, bf16[1344,512]{1,0:T(8,128)(2,1)S(1)}, f32[2,256,128]{2,1,0:T(8,128)S(1)}, f32[128,128]{1,0:T(8,128)S(1)}) custom-call(s32[4]{0:T(128)} %prefix_in.1, bf16[128,512]{1,0:T(8,128)(2,1)} %query_in.1, bf16[128,256]{1,0:T(8,128)(2,1)} %key_in.1, ...), custom_call_target="tpu_custom_call" | custom-call | tf_op jit(solution)/shard_map/own_scores/pallas_call | solution.py:175
  6.2 2.0 %collective-permute-done = bf16[1,128,256]{2,1,0:T(8,128)(2,1)S(1)} collective-permute-done((bf16[1,128,256]{2,1,0:T(8,128)(2,1)}, bf16[1,128,256]{2,1,0:T(8,128)(2,1)S(1)}, u32[]{:S(2)}, u32[]{:S(2)}) %collective-permute-start) | collective-permute-done | bytes 65568 | tf_op jit(solution)/shard_map/ppermute | solution.py:36
  8.2 0.4 %weigh.1 = (bf16[2,256,256]{2,1,0:T(8,128)(2,1)S(1)}, f32[2,256,128]{2,1,0:T(8,128)S(1)}) custom-call(bf16[128,512]{1,0:T(8,128)(2,1)S(1)} %get-tuple-element.20.query_ref, f32[2,256,128]{2,1,0:T(8,128)S(1)} %get-tuple-element.21.score_ref, f32[128,128]{1,0:T(8,128)S(1)} %get-tuple-element.22.bias_ref, bf16[128,256]{1,0:T(8,128)(2,1)S(1)} %bitcast.19), custom_call_target="tpu_custom_call" | custom-call | tf_op jit(solution)/shard_map/weigh/pallas_call | solution.py:196
  8.6 0.8 %collective-permute-done.1 = bf16[1,128,256]{2,1,0:T(8,128)(2,1)S(1)} collective-permute-done((bf16[1,128,256]{2,1,0:T(8,128)(2,1)}, bf16[1,128,256]{2,1,0:T(8,128)(2,1)S(1)}, u32[]{:S(2)}, u32[]{:S(2)}) %collective-permute-start.1) | collective-permute-done | bytes 65568 | tf_op jit(solution)/shard_map/ppermute | solution.py:36
  9.4 0.2 attend.1
  9.7 0.1 collective-permute-start.2
  9.7 0.0 copy-done.1
  9.8 0.9 %collective-permute-start.7 = (bf16[64,512]{1,0:T(8,128)(2,1)S(1)}, bf16[64,512]{1,0:T(8,128)(2,1)S(1)}, u32[]{:S(2)}, u32[]{:S(2)}) collective-permute-start(bf16[64,512]{1,0:T(8,128)(2,1)S(1)} %get-tuple-element.27), channel_id=1, source_target_pairs={{0,9},{1,8},{2,11},{3,10},{4,13},{5,12},{6,15},{7,14},{8,1},{9,0},... | collective-permute-start | bytes 196616 | tf_op jit(solution)/shard_map/ppermute | solution.py:51
  10.7 2.2 %collective-permute-start.6 = (bf16[64,512]{1,0:T(8,128)(2,1)S(1)}, bf16[64,512]{1,0:T(8,128)(2,1)S(1)}, u32[]{:S(2)}, u32[]{:S(2)}) collective-permute-start(bf16[64,512]{1,0:T(8,128)(2,1)S(1)} %get-tuple-element.26), channel_id=1, source_target_pairs={{0,8},{4,12},{8,0},{12,4},{1,9},{5,13},{9,1},{13,5},{2,10},{6,14},... | collective-permute-start | bytes 196616 | tf_op jit(solution)/shard_map/ppermute | solution.py:41
  12.8 0.0 collective-permute-done.2
  12.9 0.1 collective-permute-start.5
  12.9 0.0 collective-permute-done.3.refs_2_.refs_3_
  13.0 0.9 %project.3 = (bf16[1,32,1344]{2,1,0:T(8,128)(2,1)S(1)}, f32[1,32,1344]{2,1,0:T(8,128)S(1)}) custom-call(bf16[2,64,512]{2,1,0:T(8,128)(2,1)S(1)} %pad_maximum_fusion.refs_0_, bf16[1344,512]{1,0:T(8,128)(2,1)S(1)} %get-tuple-element.28.refs_1_.refs_2_, bf16[1344,512]{1,0:T(8,128)(2,1)S(1)} %collective-permute-done.3.refs_2_.refs_3_), custom_call_target="tpu_custom_call" | custom-call | flops 3000000000 | tf_op jit(solution)/shard_map/project/pallas_call | solution.py:248
  13.9 1.6 %collective-permute-start.4 = (bf16[1,32,1344]{2,1,0:T(8,128)(2,1)S(1)}, bf16[1,32,1344]{2,1,0:T(8,128)(2,1)S(1)}, u32[]{:S(2)}, u32[]{:S(2)}) collective-permute-start(bf16[1,32,1344]{2,1,0:T(8,128)(2,1)S(1)} %get-tuple-element.30._.refs_4_), channel_id=1, source_target_pairs={{0,2},{1,3},{2,0},{3,1},{4,6},{5,7},{6,4},{7,5},{8,10},{9,11},{10,... | collective-permute-start | bytes 258056 | tf_op jit(solution)/shard_map/ppermute | solution.py:41
  15.5 3.1 %collective-permute-done.6.own_ref = bf16[64,512]{1,0:T(8,128)(2,1)S(1)} collective-permute-done((bf16[64,512]{1,0:T(8,128)(2,1)S(1)}, bf16[64,512]{1,0:T(8,128)(2,1)S(1)}, u32[]{:S(2)}, u32[]{:S(2)}) %collective-permute-start.6) | collective-permute-done | bytes 65568 | tf_op jit(solution)/shard_map/ppermute | solution.py:41
  18.6 0.0 collective-permute-done.7.other_ref
  18.6 0.1 collective-permute-start.11
  18.7 1.3 %collective-permute-done.5.refs_0_ = bf16[2,64,512]{2,1,0:T(8,128)(2,1)S(1)} collective-permute-done((bf16[2,64,512]{2,1,0:T(8,128)(2,1)S(1)}, bf16[2,64,512]{2,1,0:T(8,128)(2,1)S(1)}, u32[]{:S(2)}, u32[]{:S(2)}) %collective-permute-start.5) | collective-permute-done | bytes 131104 | tf_op jit(solution)/shard_map/ppermute | solution.py:41
  19.9 1.0 %project.4 = (bf16[2,32,1344]{2,1,0:T(8,128)(2,1)S(1)}, f32[2,32,1344]{2,1,0:T(8,128)S(1)}) custom-call(bf16[2,64,512]{2,1,0:T(8,128)(2,1)S(1)} %collective-permute-done.5.refs_0_, bf16[2,64,512]{2,1,0:T(8,128)(2,1)S(1)} %stack.13.refs_1_, bf16[1344,512]{1,0:T(8,128)(2,1)S(1)} %get-tuple-element.28.refs_1_.refs_2_, ...), custom_call_target="tpu_custom_call" | custom-call | flops 3000000000 | tf_op jit(solution)/shard_map/project/pallas_call | solution.py:248
  21.0 1.6 %collective-permute-start.8 = (bf16[2,32,1344]{2,1,0:T(8,128)(2,1)S(1)}, bf16[2,32,1344]{2,1,0:T(8,128)(2,1)S(1)}, u32[]{:S(2)}, u32[]{:S(2)}) collective-permute-start(bf16[2,32,1344]{2,1,0:T(8,128)(2,1)S(1)} %get-tuple-element.32.refs_3_), channel_id=1, source_target_pairs={{0,2},{1,3},{2,0},{3,1},{4,6},{5,7},{6,4},{7,5},{8,10},{9,11},{10,... | collective-permute-start | bytes 516104 | tf_op jit(solution)/shard_map/ppermute | solution.py:41
  22.5 1.5 %collective-permute-done.11.refs_0_ = bf16[2,64,512]{2,1,0:T(8,128)(2,1)S(1)} collective-permute-done((bf16[2,64,512]{2,1,0:T(8,128)(2,1)S(1)}, bf16[2,64,512]{2,1,0:T(8,128)(2,1)S(1)}, u32[]{:S(2)}, u32[]{:S(2)}) %collective-permute-start.11) | collective-permute-done | bytes 131104 | tf_op jit(solution)/shard_map/ppermute | solution.py:41
  24.1 0.9 %project.5 = (bf16[1,32,1344]{2,1,0:T(8,128)(2,1)S(1)}, f32[1,32,1344]{2,1,0:T(8,128)S(1)}) custom-call(bf16[2,64,512]{2,1,0:T(8,128)(2,1)S(1)} %collective-permute-done.11.refs_0_, bf16[1344,512]{1,0:T(8,128)(2,1)S(1)} %get-tuple-element.28.refs_1_.refs_2_, bf16[1344,512]{1,0:T(8,128)(2,1)S(1)} %collective-permute-done.3.refs_2_.refs_3_, ...), custom_call_target="tpu_custom_call" | custom-call | flops 3000000000 | tf_op jit(solution)/shard_map/project/pallas_call | solution.py:248
  25.0 0.0 copy-start
  25.0 1.6 %collective-permute-start.12 = (bf16[1,32,1344]{2,1,0:T(8,128)(2,1)S(1)}, bf16[1,32,1344]{2,1,0:T(8,128)(2,1)S(1)}, u32[]{:S(2)}, u32[]{:S(2)}) collective-permute-start(bf16[1,32,1344]{2,1,0:T(8,128)(2,1)S(1)} %get-tuple-element.34), channel_id=1, source_target_pairs={{0,2},{1,3},{2,0},{3,1},{4,6},{5,7},{6,4},{7,5},{8,10},{9,11},{10,... | collective-permute-start | bytes 258056 | tf_op jit(solution)/shard_map/ppermute | solution.py:41
  26.6 0.1 collective-permute-done.8
  26.7 2.8 %collective-permute-start.10 = (bf16[32,1344]{1,0:T(8,128)(2,1)S(1)}, bf16[32,1344]{1,0:T(8,128)(2,1)S(1)}, u32[]{:S(2)}, u32[]{:S(2)}) collective-permute-start(bf16[32,1344]{1,0:T(8,128)(2,1)S(1)} %get-tuple-element.35._), channel_id=1, source_target_pairs={{0,8},{4,12},{8,0},{12,4},{1,9},{5,13},{9,1},{13,5},{2,10},{6,14},... | collective-permute-start | bytes 258056 | tf_op jit(solution)/shard_map/ppermute | solution.py:41
  29.5 0.4 %collective-permute-start.9 = (bf16[32,1344]{1,0:T(8,128)(2,1)S(1)}, bf16[32,1344]{1,0:T(8,128)(2,1)S(1)}, u32[]{:S(2)}, u32[]{:S(2)}) collective-permute-start(bf16[32,1344]{1,0:T(8,128)(2,1)S(1)} %finish.1), channel_id=1, source_target_pairs={{0,4},{4,0},{8,12},{12,8},{1,5},{5,1},{9,13},{13,9},{2,6},{6,2},{1... | collective-permute-start | bytes 258056 | tf_op jit(solution)/shard_map/ppermute | solution.py:41
  30.0 0.0 collective-permute-done.12
  30.0 2.2 %collective-permute-start.13 = (bf16[32,1344]{1,0:T(8,128)(2,1)S(1)}, bf16[32,1344]{1,0:T(8,128)(2,1)S(1)}, u32[]{:S(2)}, u32[]{:S(2)}) collective-permute-start(bf16[32,1344]{1,0:T(8,128)(2,1)S(1)} %fusion.1), channel_id=1, source_target_pairs={{0,12},{4,8},{8,4},{12,0},{1,13},{5,9},{9,5},{13,1},{2,14},{6,10},... | collective-permute-start | bytes 258056 | tf_op jit(solution)/shard_map/ppermute | solution.py:41
  32.1 0.0 collective-permute-done.4
  32.2 0.1 squares.2.refs_2_
  32.3 2.8 %collective-permute-done.9.refs_0_.refs_1_ = bf16[32,1344]{1,0:T(8,128)(2,1)S(1)} collective-permute-done((bf16[32,1344]{1,0:T(8,128)(2,1)S(1)}, bf16[32,1344]{1,0:T(8,128)(2,1)S(1)}, u32[]{:S(2)}, u32[]{:S(2)}) %collective-permute-start.9) | collective-permute-done | bytes 86048 | tf_op jit(solution)/shard_map/ppermute | solution.py:41
  35.0 0.0 collective-permute-done.10.refs_1_.refs_2_
  35.0 0.2 squares.3.refs_4_
  35.2 1.3 %collective-permute-done.13.refs_3_ = bf16[32,1344]{1,0:T(8,128)(2,1)S(1)} collective-permute-done((bf16[32,1344]{1,0:T(8,128)(2,1)S(1)}, bf16[32,1344]{1,0:T(8,128)(2,1)S(1)}, u32[]{:S(2)}, u32[]{:S(2)}) %collective-permute-start.13) | collective-permute-done | bytes 86048 | tf_op jit(solution)/shard_map/ppermute | solution.py:41
  36.5 0.0 copy-done
  36.5 1.1 %norm.1 = bf16[32,5376]{1,0:T(8,128)(2,1)} custom-call(f32[32,1344]{1,0:T(8,128)S(1)} %add_bitcast_fusion.refs_0_, bf16[32,1344]{1,0:T(8,128)(2,1)S(1)} %collective-permute-done.9.refs_0_.refs_1_, bf16[32,1344]{1,0:T(8,128)(2,1)S(1)} %collective-permute-done.10.refs_1_.refs_2_, bf16[32,1344]{1,0:T(8,128)(2,1)S(1)} %collective-permute-done.13.refs_3_, ...), custom_call_target="tpu_custom_call" | custom-call | tf_op jit(solution)/shard_map/norm/pallas_call | solution.py:345
  (8 shorter events, 0.1 us)
Async XLA Ops:
  0.0 13.0 %collective-permute-start.3 = (bf16[1344,512]{1,0:T(8,128)(2,1)}, bf16[1344,512]{1,0:T(8,128)(2,1)S(1)}, u32[]{:S(2)}, u32[]{:S(2)}) collective-permute-start(bf16[1344,512]{1,0:T(8,128)(2,1)} %bitcast.20), channel_id=1, source_target_pairs={{0,1},{1,0},{2,3},{3,2},{4,5},{5,4},{6,7},{7,6},{8,9},{9,8},{10,11... | collective-permute-start | bytes 4128776 | tf_op jit(solution)/shard_map/ppermute | solution.py:41
  0.5 7.7 %collective-permute-start = (bf16[1,128,256]{2,1,0:T(8,128)(2,1)}, bf16[1,128,256]{2,1,0:T(8,128)(2,1)S(1)}, u32[]{:S(2)}, u32[]{:S(2)}) collective-permute-start(bf16[1,128,256]{2,1,0:T(8,128)(2,1)} %bitcast.22), channel_id=1, source_target_pairs={{0,4},{4,8},{8,12},{12,0},{1,5},{5,9},{9,13},{13,1},{2,6},{6,10},{... | collective-permute-start | bytes 196616 | tf_op jit(solution)/shard_map/ppermute | solution.py:36
  3.0 6.7 %copy-start.1 = (f32[5376]{0:T(1024)S(1)}, f32[5376]{0:T(1024)}, u32[]{:S(2)}) copy-start(f32[5376]{0:T(1024)} %param.13) | copy-start | bytes 64516
  3.0 6.4 %collective-permute-start.1 = (bf16[1,128,256]{2,1,0:T(8,128)(2,1)}, bf16[1,128,256]{2,1,0:T(8,128)(2,1)S(1)}, u32[]{:S(2)}, u32[]{:S(2)}) collective-permute-start(bf16[1,128,256]{2,1,0:T(8,128)(2,1)} %bitcast.23), channel_id=1, source_target_pairs={{0,4},{4,8},{8,12},{12,0},{1,5},{5,9},{9,13},{13,1},{2,6},{6,10},{... | collective-permute-start | bytes 196616 | tf_op jit(solution)/shard_map/ppermute | solution.py:36
  9.7 3.2 %collective-permute-start.2 = (bf16[64,512]{1,0:T(8,128)(2,1)S(1)}, bf16[64,512]{1,0:T(8,128)(2,1)S(1)}, u32[]{:S(2)}, u32[]{:S(2)}) collective-permute-start(bf16[64,512]{1,0:T(8,128)(2,1)S(1)} %get-tuple-element.27), channel_id=1, source_target_pairs={{0,1},{1,0},{2,3},{3,2},{4,5},{5,4},{6,7},{7,6},{8,9},{9,8},{10,11... | collective-permute-start | bytes 196616 | tf_op jit(solution)/shard_map/ppermute | solution.py:41
  9.8 8.8 %collective-permute-start.7 = (bf16[64,512]{1,0:T(8,128)(2,1)S(1)}, bf16[64,512]{1,0:T(8,128)(2,1)S(1)}, u32[]{:S(2)}, u32[]{:S(2)}) collective-permute-start(bf16[64,512]{1,0:T(8,128)(2,1)S(1)} %get-tuple-element.27), channel_id=1, source_target_pairs={{0,9},{1,8},{2,11},{3,10},{4,13},{5,12},{6,15},{7,14},{8,1},{9,0},... | collective-permute-start | bytes 196616 | tf_op jit(solution)/shard_map/ppermute | solution.py:51
  10.7 7.9 %collective-permute-start.6 = (bf16[64,512]{1,0:T(8,128)(2,1)S(1)}, bf16[64,512]{1,0:T(8,128)(2,1)S(1)}, u32[]{:S(2)}, u32[]{:S(2)}) collective-permute-start(bf16[64,512]{1,0:T(8,128)(2,1)S(1)} %get-tuple-element.26), channel_id=1, source_target_pairs={{0,8},{4,12},{8,0},{12,4},{1,9},{5,13},{9,1},{13,5},{2,10},{6,14},... | collective-permute-start | bytes 196616 | tf_op jit(solution)/shard_map/ppermute | solution.py:41
  12.9 7.1 %collective-permute-start.5 = (bf16[2,64,512]{2,1,0:T(8,128)(2,1)S(1)}, bf16[2,64,512]{2,1,0:T(8,128)(2,1)S(1)}, u32[]{:S(2)}, u32[]{:S(2)}) collective-permute-start(bf16[2,64,512]{2,1,0:T(8,128)(2,1)S(1)} %pad_maximum_fusion.refs_0_), channel_id=1, source_target_pairs={{0,4},{4,0},{8,12},{12,8},{1,5},{5,1},{9,13},{13,9},{2,6},{6,2},{1... | collective-permute-start | bytes 393224 | tf_op jit(solution)/shard_map/ppermute | solution.py:41
  13.9 18.2 %collective-permute-start.4 = (bf16[1,32,1344]{2,1,0:T(8,128)(2,1)S(1)}, bf16[1,32,1344]{2,1,0:T(8,128)(2,1)S(1)}, u32[]{:S(2)}, u32[]{:S(2)}) collective-permute-start(bf16[1,32,1344]{2,1,0:T(8,128)(2,1)S(1)} %get-tuple-element.30._.refs_4_), channel_id=1, source_target_pairs={{0,2},{1,3},{2,0},{3,1},{4,6},{5,7},{6,4},{7,5},{8,10},{9,11},{10,... | collective-permute-start | bytes 258056 | tf_op jit(solution)/shard_map/ppermute | solution.py:41
  18.6 5.5 %collective-permute-start.11 = (bf16[2,64,512]{2,1,0:T(8,128)(2,1)S(1)}, bf16[2,64,512]{2,1,0:T(8,128)(2,1)S(1)}, u32[]{:S(2)}, u32[]{:S(2)}) collective-permute-start(bf16[2,64,512]{2,1,0:T(8,128)(2,1)S(1)} %stack.13.refs_1_), channel_id=1, source_target_pairs={{0,4},{4,0},{8,12},{12,8},{1,5},{5,1},{9,13},{13,9},{2,6},{6,2},{1... | collective-permute-start | bytes 393224 | tf_op jit(solution)/shard_map/ppermute | solution.py:41
  21.0 5.7 %collective-permute-start.8 = (bf16[2,32,1344]{2,1,0:T(8,128)(2,1)S(1)}, bf16[2,32,1344]{2,1,0:T(8,128)(2,1)S(1)}, u32[]{:S(2)}, u32[]{:S(2)}) collective-permute-start(bf16[2,32,1344]{2,1,0:T(8,128)(2,1)S(1)} %get-tuple-element.32.refs_3_), channel_id=1, source_target_pairs={{0,2},{1,3},{2,0},{3,1},{4,6},{5,7},{6,4},{7,5},{8,10},{9,11},{10,... | collective-permute-start | bytes 516104 | tf_op jit(solution)/shard_map/ppermute | solution.py:41
  25.0 11.5 %copy-start = (bf16[32,5376]{1,0:T(8,128)(2,1)S(1)}, bf16[32,5376]{1,0:T(8,128)(2,1)}, u32[]{:S(2)}) copy-start(bf16[32,5376]{1,0:T(8,128)(2,1)} %refs_5_.1) | copy-start | bytes 1032196
  25.0 4.9 %collective-permute-start.12 = (bf16[1,32,1344]{2,1,0:T(8,128)(2,1)S(1)}, bf16[1,32,1344]{2,1,0:T(8,128)(2,1)S(1)}, u32[]{:S(2)}, u32[]{:S(2)}) collective-permute-start(bf16[1,32,1344]{2,1,0:T(8,128)(2,1)S(1)} %get-tuple-element.34), channel_id=1, source_target_pairs={{0,2},{1,3},{2,0},{3,1},{4,6},{5,7},{6,4},{7,5},{8,10},{9,11},{10,... | collective-permute-start | bytes 258056 | tf_op jit(solution)/shard_map/ppermute | solution.py:41
  26.7 8.3 %collective-permute-start.10 = (bf16[32,1344]{1,0:T(8,128)(2,1)S(1)}, bf16[32,1344]{1,0:T(8,128)(2,1)S(1)}, u32[]{:S(2)}, u32[]{:S(2)}) collective-permute-start(bf16[32,1344]{1,0:T(8,128)(2,1)S(1)} %get-tuple-element.35._), channel_id=1, source_target_pairs={{0,8},{4,12},{8,0},{12,4},{1,9},{5,13},{9,1},{13,5},{2,10},{6,14},... | collective-permute-start | bytes 258056 | tf_op jit(solution)/shard_map/ppermute | solution.py:41
  29.5 5.5 %collective-permute-start.9 = (bf16[32,1344]{1,0:T(8,128)(2,1)S(1)}, bf16[32,1344]{1,0:T(8,128)(2,1)S(1)}, u32[]{:S(2)}, u32[]{:S(2)}) collective-permute-start(bf16[32,1344]{1,0:T(8,128)(2,1)S(1)} %finish.1), channel_id=1, source_target_pairs={{0,4},{4,0},{8,12},{12,8},{1,5},{5,1},{9,13},{13,9},{2,6},{6,2},{1... | collective-permute-start | bytes 258056 | tf_op jit(solution)/shard_map/ppermute | solution.py:41
  30.0 6.5 %collective-permute-start.13 = (bf16[32,1344]{1,0:T(8,128)(2,1)S(1)}, bf16[32,1344]{1,0:T(8,128)(2,1)S(1)}, u32[]{:S(2)}, u32[]{:S(2)}) collective-permute-start(bf16[32,1344]{1,0:T(8,128)(2,1)S(1)} %fusion.1), channel_id=1, source_target_pairs={{0,12},{4,8},{8,4},{12,0},{1,13},{5,9},{9,5},{13,1},{2,14},{6,10},... | collective-permute-start | bytes 258056 | tf_op jit(solution)/shard_map/ppermute | solution.py:41
where the time goes:
time: 37.7 us; the launch traced here: 37.6 us
  starting transfers between devices  17.9 us (47%)
  waiting for transfers between devices  13 us (34%)
  Pallas kernels  6.46 us (17%)
    ppermute x11, starting transfers between devices, exchanged(): return lax.ppermute(value, axis, [(at, at ^ flip) for at in range(count)])  12.9 us
    ppermute x11, waiting for transfers between devices, exchanged(): return lax.ppermute(value, axis, [(at, at ^ flip) for at in range(count)])  10.1 us
    ppermute x2, starting transfers between devices, rotated(): lax.ppermute(value, axis, [(at, (at + steps) % count) for at in range(cou...  4.15 us
    pallas_call x3, Pallas kernels, project(): pl.pallas_call(functools.partial(project_kernel, [len(chunk) for chunk in...  2.89 us
    ppermute x2, waiting for transfers between devices, rotated(): lax.ppermute(value, axis, [(at, (at + steps) % count) for at in range(cou...  2.88 us
    pallas_call x1, Pallas kernels, attend(): pl.pallas_call(own_kernel, out_shape=(like(queries), like(values), like(t...  1.54 us
    pallas_call x1, Pallas kernels, norm(): pl.pallas_call(functools.partial(norm_kernel, len(pieces)), out_shape=jax...  1.12 us
    ppermute x1, starting transfers between devices, crossed(): return lax.ppermute(value, ('section', 'head'), pairs)  0.88 us
  transfers between devices with their start and end apart: 14, of which 8 were waited for; matrix products, arithmetic and copies ran while one was open for 0% of the time, Pallas kernels for 14%

commit v1 on v0

--- a/solution.py
+++ b/solution.py
@@ -316,7 +316,7 @@
 
 def norm_kernel(count, *refs):
     piece_refs = refs[:count]
-    squares_ref, residual_ref, gain_ref, out_ref, piece_ref = refs[count:]
+    squares_ref, residual_ref, gain_ref, out_ref, piece_ref, made_ref, sems = refs[count:]
     width = piece_ref.shape[2]
     for at, moved_ref in enumerate(piece_refs):
         piece_ref[at] = moved_ref[...].astype(jnp.float32)
@@ -324,10 +324,21 @@
     square = squares_ref[:, :1] + jnp.sum(last * last, axis=-1, keepdims=True)
     scale = lax.rsqrt(square / (count * width) + norm_eps)
     section_index = lax.axis_index("section")
-    for at in range(count):
-        place = slice(at * width, (at + 1) * width)
-        normed = piece_ref[section_index ^ at] * scale * gain_ref[:, place]
-        out_ref[:, place] = (residual_ref[:, place].astype(jnp.float32) + normed).astype(jnp.bfloat16)
+    steps = sems.shape[0]
+    together = count // steps
+    stores = []
+    for step in range(steps):
+        first = step * together
+        place = slice(first * width, (first + together) * width)
+        wide = [piece_ref[section_index ^ at] for at in range(first, first + together)]
+        normed = jnp.concatenate(wide, axis=1) * scale * gain_ref[:, place]
+        made_ref[:, place] = (residual_ref[:, place].astype(jnp.float32) + normed).astype(jnp.bfloat16)
+        stores.append(
+            pltpu.make_async_copy(made_ref.at[:, place], out_ref.at[:, place], sems.at[step])
+        )
+        stores[-1].start()
+    for store in stores:
+        store.wait()
 
 
 def last_flip(section_total):
@@ -342,12 +353,18 @@
     early = None
     for group in section_flips(len(pieces))[:-1]:
         early = squares([pieces[flip] for flip in group], early)
+    count, width = len(pieces), pieces[0].shape[1]
+    steps = 2 if count * width % (2 * HEAD_SIZE) == 0 else 1
     return pl.pallas_call(
-        functools.partial(norm_kernel, len(pieces)),
+        functools.partial(norm_kernel, count),
         out_shape=jax.ShapeDtypeStruct(residual.shape, jnp.bfloat16),
-        in_specs=[in_vmem] * (len(pieces) + 3),
-        out_specs=in_vmem,
-        scratch_shapes=[pltpu.VMEM((len(pieces), *pieces[0].shape), jnp.float32)],
+        in_specs=[in_vmem] * (count + 3),
+        out_specs=in_hbm,
+        scratch_shapes=[
+            pltpu.VMEM((count, *pieces[0].shape), jnp.float32),
+            pltpu.VMEM(residual.shape, jnp.bfloat16),
+            pltpu.SemaphoreType.DMA((steps,)),
+        ],
         compiler_params=pltpu.CompilerParams(vmem_limit_bytes=vmem_bytes),
         cost_estimate=no_cost,
         name="norm",

time: 37.7 us -> 37.7 us (level)
  no operation moved by 1% of the time
where the time goes in v1:
time: 37.7 us; the launch traced here: 37.5 us
  starting transfers between devices  17.9 us (47%)
  waiting for transfers between devices  13 us (34%)
  Pallas kernels  6.4 us (17%)
    ppermute x11, starting transfers between devices, exchanged(): return lax.ppermute(value, axis, [(at, at ^ flip) for at in range(count)])  12.9 us
    ppermute x11, waiting for transfers between devices, exchanged(): return lax.ppermute(value, axis, [(at, at ^ flip) for at in range(count)])  10.1 us
    ppermute x2, starting transfers between devices, rotated(): lax.ppermute(value, axis, [(at, (at + steps) % count) for at in range(cou...  4.15 us
    pallas_call x3, Pallas kernels, project(): pl.pallas_call(functools.partial(project_kernel, [len(chunk) for chunk in...  2.89 us
    ppermute x2, waiting for transfers between devices, rotated(): lax.ppermute(value, axis, [(at, (at + steps) % count) for at in range(cou...  2.88 us
    pallas_call x1, Pallas kernels, attend(): pl.pallas_call(own_kernel, out_shape=(like(queries), like(values), like(t...  1.54 us
    pallas_call x1, Pallas kernels, norm(): pl.pallas_call(functools.partial(norm_kernel, count), out_shape=jax.Shape...  1.06 us
    ppermute x1, starting transfers between devices, crossed(): return lax.ppermute(value, ('section', 'head'), pairs)  0.88 us
  transfers between devices with their start and end apart: 14, of which 8 were waited for; matrix products, arithmetic and copies ran while one was open for 0% of the time, Pallas kernels for 14%

profile of v1, /device:TPU:0, one launch (start us, length us, event | category | flops | bytes accessed | tf_op | source)
XLA Modules:
  0.0 37.5 jit_solution(1300510472874817568)
XLA Ops:
  0.0 0.5 %collective-permute-start.3 = (bf16[1344,512]{1,0:T(8,128)(2,1)}, bf16[1344,512]{1,0:T(8,128)(2,1)S(1)}, u32[]{:S(2)}, u32[]{:S(2)}) collective-permute-start(bf16[1344,512]{1,0:T(8,128)(2,1)} %bitcast.20), channel_id=1, source_target_pairs={{0,1},{1,0},{2,3},{3,2},{4,5},{5,4},{6,7},{7,6},{8,9},{9,8},{10,11... | collective-permute-start | bytes 4128776 | tf_op jit(solution)/shard_map/ppermute | solution.py:41
  0.5 2.6 %collective-permute-start = (bf16[1,128,256]{2,1,0:T(8,128)(2,1)}, bf16[1,128,256]{2,1,0:T(8,128)(2,1)S(1)}, u32[]{:S(2)}, u32[]{:S(2)}) collective-permute-start(bf16[1,128,256]{2,1,0:T(8,128)(2,1)} %bitcast.22), channel_id=1, source_target_pairs={{0,4},{4,8},{8,12},{12,0},{1,5},{5,9},{9,13},{13,1},{2,6},{6,10},{... | collective-permute-start | bytes 196616 | tf_op jit(solution)/shard_map/ppermute | solution.py:36
  3.0 0.0 copy-start.1
  3.0 1.6 %collective-permute-start.1 = (bf16[1,128,256]{2,1,0:T(8,128)(2,1)}, bf16[1,128,256]{2,1,0:T(8,128)(2,1)S(1)}, u32[]{:S(2)}, u32[]{:S(2)}) collective-permute-start(bf16[1,128,256]{2,1,0:T(8,128)(2,1)} %bitcast.23), channel_id=1, source_target_pairs={{0,4},{4,8},{8,12},{12,0},{1,5},{5,9},{9,13},{13,1},{2,6},{6,10},{... | collective-permute-start | bytes 196616 | tf_op jit(solution)/shard_map/ppermute | solution.py:36
  4.6 1.5 %own_scores.1 = (bf16[128,512]{1,0:T(8,128)(2,1)S(1)}, bf16[128,256]{1,0:T(8,128)(2,1)S(1)}, bf16[1344,512]{1,0:T(8,128)(2,1)S(1)}, f32[2,256,128]{2,1,0:T(8,128)S(1)}, f32[128,128]{1,0:T(8,128)S(1)}) custom-call(s32[4]{0:T(128)} %prefix_in.1, bf16[128,512]{1,0:T(8,128)(2,1)} %query_in.1, bf16[128,256]{1,0:T(8,128)(2,1)} %key_in.1, ...), custom_call_target="tpu_custom_call" | custom-call | tf_op jit(solution)/shard_map/own_scores/pallas_call | solution.py:175
  6.2 2.0 %collective-permute-done = bf16[1,128,256]{2,1,0:T(8,128)(2,1)S(1)} collective-permute-done((bf16[1,128,256]{2,1,0:T(8,128)(2,1)}, bf16[1,128,256]{2,1,0:T(8,128)(2,1)S(1)}, u32[]{:S(2)}, u32[]{:S(2)}) %collective-permute-start) | collective-permute-done | bytes 65568 | tf_op jit(solution)/shard_map/ppermute | solution.py:36
  8.2 0.4 %weigh.1 = (bf16[2,256,256]{2,1,0:T(8,128)(2,1)S(1)}, f32[2,256,128]{2,1,0:T(8,128)S(1)}) custom-call(bf16[128,512]{1,0:T(8,128)(2,1)S(1)} %get-tuple-element.20.query_ref, f32[2,256,128]{2,1,0:T(8,128)S(1)} %get-tuple-element.21.score_ref, f32[128,128]{1,0:T(8,128)S(1)} %get-tuple-element.22.bias_ref, bf16[128,256]{1,0:T(8,128)(2,1)S(1)} %bitcast.19), custom_call_target="tpu_custom_call" | custom-call | tf_op jit(solution)/shard_map/weigh/pallas_call | solution.py:196
  8.6 0.8 %collective-permute-done.1 = bf16[1,128,256]{2,1,0:T(8,128)(2,1)S(1)} collective-permute-done((bf16[1,128,256]{2,1,0:T(8,128)(2,1)}, bf16[1,128,256]{2,1,0:T(8,128)(2,1)S(1)}, u32[]{:S(2)}, u32[]{:S(2)}) %collective-permute-start.1) | collective-permute-done | bytes 65568 | tf_op jit(solution)/shard_map/ppermute | solution.py:36
  9.4 0.2 attend.1
  9.7 0.1 collective-permute-start.2
  9.7 0.0 copy-done.1
  9.8 0.9 %collective-permute-start.7 = (bf16[64,512]{1,0:T(8,128)(2,1)S(1)}, bf16[64,512]{1,0:T(8,128)(2,1)S(1)}, u32[]{:S(2)}, u32[]{:S(2)}) collective-permute-start(bf16[64,512]{1,0:T(8,128)(2,1)S(1)} %get-tuple-element.27), channel_id=1, source_target_pairs={{0,9},{1,8},{2,11},{3,10},{4,13},{5,12},{6,15},{7,14},{8,1},{9,0},... | collective-permute-start | bytes 196616 | tf_op jit(solution)/shard_map/ppermute | solution.py:51
  10.7 2.2 %collective-permute-start.6 = (bf16[64,512]{1,0:T(8,128)(2,1)S(1)}, bf16[64,512]{1,0:T(8,128)(2,1)S(1)}, u32[]{:S(2)}, u32[]{:S(2)}) collective-permute-start(bf16[64,512]{1,0:T(8,128)(2,1)S(1)} %get-tuple-element.26), channel_id=1, source_target_pairs={{0,8},{4,12},{8,0},{12,4},{1,9},{5,13},{9,1},{13,5},{2,10},{6,14},... | collective-permute-start | bytes 196616 | tf_op jit(solution)/shard_map/ppermute | solution.py:41
  12.8 0.0 collective-permute-done.2
  12.9 0.1 collective-permute-start.5
  12.9 0.0 collective-permute-done.3.refs_2_.refs_3_
  13.0 0.9 %project.3 = (bf16[1,32,1344]{2,1,0:T(8,128)(2,1)S(1)}, f32[1,32,1344]{2,1,0:T(8,128)S(1)}) custom-call(bf16[2,64,512]{2,1,0:T(8,128)(2,1)S(1)} %pad_maximum_fusion.refs_0_, bf16[1344,512]{1,0:T(8,128)(2,1)S(1)} %get-tuple-element.28.refs_1_.refs_2_, bf16[1344,512]{1,0:T(8,128)(2,1)S(1)} %collective-permute-done.3.refs_2_.refs_3_), custom_call_target="tpu_custom_call" | custom-call | flops 3000000000 | tf_op jit(solution)/shard_map/project/pallas_call | solution.py:248
  13.9 1.6 %collective-permute-start.4 = (bf16[1,32,1344]{2,1,0:T(8,128)(2,1)S(1)}, bf16[1,32,1344]{2,1,0:T(8,128)(2,1)S(1)}, u32[]{:S(2)}, u32[]{:S(2)}) collective-permute-start(bf16[1,32,1344]{2,1,0:T(8,128)(2,1)S(1)} %get-tuple-element.30._.refs_4_), channel_id=1, source_target_pairs={{0,2},{1,3},{2,0},{3,1},{4,6},{5,7},{6,4},{7,5},{8,10},{9,11},{10,... | collective-permute-start | bytes 258056 | tf_op jit(solution)/shard_map/ppermute | solution.py:41
  15.5 3.1 %collective-permute-done.6.own_ref = bf16[64,512]{1,0:T(8,128)(2,1)S(1)} collective-permute-done((bf16[64,512]{1,0:T(8,128)(2,1)S(1)}, bf16[64,512]{1,0:T(8,128)(2,1)S(1)}, u32[]{:S(2)}, u32[]{:S(2)}) %collective-permute-start.6) | collective-permute-done | bytes 65568 | tf_op jit(solution)/shard_map/ppermute | solution.py:41
  18.6 0.0 collective-permute-done.7.other_ref
  18.6 0.1 collective-permute-start.11
  18.7 1.3 %collective-permute-done.5.refs_0_ = bf16[2,64,512]{2,1,0:T(8,128)(2,1)S(1)} collective-permute-done((bf16[2,64,512]{2,1,0:T(8,128)(2,1)S(1)}, bf16[2,64,512]{2,1,0:T(8,128)(2,1)S(1)}, u32[]{:S(2)}, u32[]{:S(2)}) %collective-permute-start.5) | collective-permute-done | bytes 131104 | tf_op jit(solution)/shard_map/ppermute | solution.py:41
  19.9 1.0 %project.4 = (bf16[2,32,1344]{2,1,0:T(8,128)(2,1)S(1)}, f32[2,32,1344]{2,1,0:T(8,128)S(1)}) custom-call(bf16[2,64,512]{2,1,0:T(8,128)(2,1)S(1)} %collective-permute-done.5.refs_0_, bf16[2,64,512]{2,1,0:T(8,128)(2,1)S(1)} %stack.13.refs_1_, bf16[1344,512]{1,0:T(8,128)(2,1)S(1)} %get-tuple-element.28.refs_1_.refs_2_, ...), custom_call_target="tpu_custom_call" | custom-call | flops 3000000000 | tf_op jit(solution)/shard_map/project/pallas_call | solution.py:248
  21.0 1.6 %collective-permute-start.8 = (bf16[2,32,1344]{2,1,0:T(8,128)(2,1)S(1)}, bf16[2,32,1344]{2,1,0:T(8,128)(2,1)S(1)}, u32[]{:S(2)}, u32[]{:S(2)}) collective-permute-start(bf16[2,32,1344]{2,1,0:T(8,128)(2,1)S(1)} %get-tuple-element.32.refs_3_), channel_id=1, source_target_pairs={{0,2},{1,3},{2,0},{3,1},{4,6},{5,7},{6,4},{7,5},{8,10},{9,11},{10,... | collective-permute-start | bytes 516104 | tf_op jit(solution)/shard_map/ppermute | solution.py:41
  22.5 1.5 %collective-permute-done.11.refs_0_ = bf16[2,64,512]{2,1,0:T(8,128)(2,1)S(1)} collective-permute-done((bf16[2,64,512]{2,1,0:T(8,128)(2,1)S(1)}, bf16[2,64,512]{2,1,0:T(8,128)(2,1)S(1)}, u32[]{:S(2)}, u32[]{:S(2)}) %collective-permute-start.11) | collective-permute-done | bytes 131104 | tf_op jit(solution)/shard_map/ppermute | solution.py:41
  24.1 0.9 %project.5 = (bf16[1,32,1344]{2,1,0:T(8,128)(2,1)S(1)}, f32[1,32,1344]{2,1,0:T(8,128)S(1)}) custom-call(bf16[2,64,512]{2,1,0:T(8,128)(2,1)S(1)} %collective-permute-done.11.refs_0_, bf16[1344,512]{1,0:T(8,128)(2,1)S(1)} %get-tuple-element.28.refs_1_.refs_2_, bf16[1344,512]{1,0:T(8,128)(2,1)S(1)} %collective-permute-done.3.refs_2_.refs_3_, ...), custom_call_target="tpu_custom_call" | custom-call | flops 3000000000 | tf_op jit(solution)/shard_map/project/pallas_call | solution.py:248
  25.0 0.0 copy-start
  25.0 1.6 %collective-permute-start.12 = (bf16[1,32,1344]{2,1,0:T(8,128)(2,1)S(1)}, bf16[1,32,1344]{2,1,0:T(8,128)(2,1)S(1)}, u32[]{:S(2)}, u32[]{:S(2)}) collective-permute-start(bf16[1,32,1344]{2,1,0:T(8,128)(2,1)S(1)} %get-tuple-element.34), channel_id=1, source_target_pairs={{0,2},{1,3},{2,0},{3,1},{4,6},{5,7},{6,4},{7,5},{8,10},{9,11},{10,... | collective-permute-start | bytes 258056 | tf_op jit(solution)/shard_map/ppermute | solution.py:41
  26.6 0.1 collective-permute-done.8
  26.7 2.8 %collective-permute-start.10 = (bf16[32,1344]{1,0:T(8,128)(2,1)S(1)}, bf16[32,1344]{1,0:T(8,128)(2,1)S(1)}, u32[]{:S(2)}, u32[]{:S(2)}) collective-permute-start(bf16[32,1344]{1,0:T(8,128)(2,1)S(1)} %get-tuple-element.35._), channel_id=1, source_target_pairs={{0,8},{4,12},{8,0},{12,4},{1,9},{5,13},{9,1},{13,5},{2,10},{6,14},... | collective-permute-start | bytes 258056 | tf_op jit(solution)/shard_map/ppermute | solution.py:41
  29.5 0.4 %collective-permute-start.9 = (bf16[32,1344]{1,0:T(8,128)(2,1)S(1)}, bf16[32,1344]{1,0:T(8,128)(2,1)S(1)}, u32[]{:S(2)}, u32[]{:S(2)}) collective-permute-start(bf16[32,1344]{1,0:T(8,128)(2,1)S(1)} %finish.1), channel_id=1, source_target_pairs={{0,4},{4,0},{8,12},{12,8},{1,5},{5,1},{9,13},{13,9},{2,6},{6,2},{1... | collective-permute-start | bytes 258056 | tf_op jit(solution)/shard_map/ppermute | solution.py:41
  30.0 0.0 collective-permute-done.12
  30.0 2.2 %collective-permute-start.13 = (bf16[32,1344]{1,0:T(8,128)(2,1)S(1)}, bf16[32,1344]{1,0:T(8,128)(2,1)S(1)}, u32[]{:S(2)}, u32[]{:S(2)}) collective-permute-start(bf16[32,1344]{1,0:T(8,128)(2,1)S(1)} %fusion.1), channel_id=1, source_target_pairs={{0,12},{4,8},{8,4},{12,0},{1,13},{5,9},{9,5},{13,1},{2,14},{6,10},... | collective-permute-start | bytes 258056 | tf_op jit(solution)/shard_map/ppermute | solution.py:41
  32.1 0.0 collective-permute-done.4
  32.2 0.1 squares.2.refs_2_
  32.3 2.8 %collective-permute-done.9.refs_0_.refs_1_ = bf16[32,1344]{1,0:T(8,128)(2,1)S(1)} collective-permute-done((bf16[32,1344]{1,0:T(8,128)(2,1)S(1)}, bf16[32,1344]{1,0:T(8,128)(2,1)S(1)}, u32[]{:S(2)}, u32[]{:S(2)}) %collective-permute-start.9) | collective-permute-done | bytes 86048 | tf_op jit(solution)/shard_map/ppermute | solution.py:41
  35.0 0.0 collective-permute-done.10.refs_1_.refs_2_
  35.0 0.2 squares.3.refs_4_
  35.2 1.3 %collective-permute-done.13.refs_3_ = bf16[32,1344]{1,0:T(8,128)(2,1)S(1)} collective-permute-done((bf16[32,1344]{1,0:T(8,128)(2,1)S(1)}, bf16[32,1344]{1,0:T(8,128)(2,1)S(1)}, u32[]{:S(2)}, u32[]{:S(2)}) %collective-permute-start.13) | collective-permute-done | bytes 86048 | tf_op jit(solution)/shard_map/ppermute | solution.py:41
  36.5 0.0 copy-done
  36.5 1.1 %norm.1 = bf16[32,5376]{1,0:T(8,128)(2,1)} custom-call(f32[32,1344]{1,0:T(8,128)S(1)} %add_bitcast_fusion.refs_0_, bf16[32,1344]{1,0:T(8,128)(2,1)S(1)} %collective-permute-done.9.refs_0_.refs_1_, bf16[32,1344]{1,0:T(8,128)(2,1)S(1)} %collective-permute-done.10.refs_1_.refs_2_, bf16[32,1344]{1,0:T(8,128)(2,1)S(1)} %collective-permute-done.13.refs_3_, ...), custom_call_target="tpu_custom_call" | custom-call | tf_op jit(solution)/shard_map/norm/pallas_call | solution.py:358
  (8 shorter events, 0.1 us)
Async XLA Ops:
  0.0 13.0 %collective-permute-start.3 = (bf16[1344,512]{1,0:T(8,128)(2,1)}, bf16[1344,512]{1,0:T(8,128)(2,1)S(1)}, u32[]{:S(2)}, u32[]{:S(2)}) collective-permute-start(bf16[1344,512]{1,0:T(8,128)(2,1)} %bitcast.20), channel_id=1, source_target_pairs={{0,1},{1,0},{2,3},{3,2},{4,5},{5,4},{6,7},{7,6},{8,9},{9,8},{10,11... | collective-permute-start | bytes 4128776 | tf_op jit(solution)/shard_map/ppermute | solution.py:41
  0.5 7.7 %collective-permute-start = (bf16[1,128,256]{2,1,0:T(8,128)(2,1)}, bf16[1,128,256]{2,1,0:T(8,128)(2,1)S(1)}, u32[]{:S(2)}, u32[]{:S(2)}) collective-permute-start(bf16[1,128,256]{2,1,0:T(8,128)(2,1)} %bitcast.22), channel_id=1, source_target_pairs={{0,4},{4,8},{8,12},{12,0},{1,5},{5,9},{9,13},{13,1},{2,6},{6,10},{... | collective-permute-start | bytes 196616 | tf_op jit(solution)/shard_map/ppermute | solution.py:36
  3.0 6.7 %copy-start.1 = (f32[5376]{0:T(1024)S(1)}, f32[5376]{0:T(1024)}, u32[]{:S(2)}) copy-start(f32[5376]{0:T(1024)} %param.13) | copy-start | bytes 64516
  3.0 6.4 %collective-permute-start.1 = (bf16[1,128,256]{2,1,0:T(8,128)(2,1)}, bf16[1,128,256]{2,1,0:T(8,128)(2,1)S(1)}, u32[]{:S(2)}, u32[]{:S(2)}) collective-permute-start(bf16[1,128,256]{2,1,0:T(8,128)(2,1)} %bitcast.23), channel_id=1, source_target_pairs={{0,4},{4,8},{8,12},{12,0},{1,5},{5,9},{9,13},{13,1},{2,6},{6,10},{... | collective-permute-start | bytes 196616 | tf_op jit(solution)/shard_map/ppermute | solution.py:36
  9.7 3.2 %collective-permute-start.2 = (bf16[64,512]{1,0:T(8,128)(2,1)S(1)}, bf16[64,512]{1,0:T(8,128)(2,1)S(1)}, u32[]{:S(2)}, u32[]{:S(2)}) collective-permute-start(bf16[64,512]{1,0:T(8,128)(2,1)S(1)} %get-tuple-element.27), channel_id=1, source_target_pairs={{0,1},{1,0},{2,3},{3,2},{4,5},{5,4},{6,7},{7,6},{8,9},{9,8},{10,11... | collective-permute-start | bytes 196616 | tf_op jit(solution)/shard_map/ppermute | solution.py:41
  9.8 8.8 %collective-permute-start.7 = (bf16[64,512]{1,0:T(8,128)(2,1)S(1)}, bf16[64,512]{1,0:T(8,128)(2,1)S(1)}, u32[]{:S(2)}, u32[]{:S(2)}) collective-permute-start(bf16[64,512]{1,0:T(8,128)(2,1)S(1)} %get-tuple-element.27), channel_id=1, source_target_pairs={{0,9},{1,8},{2,11},{3,10},{4,13},{5,12},{6,15},{7,14},{8,1},{9,0},... | collective-permute-start | bytes 196616 | tf_op jit(solution)/shard_map/ppermute | solution.py:51
  10.7 7.9 %collective-permute-start.6 = (bf16[64,512]{1,0:T(8,128)(2,1)S(1)}, bf16[64,512]{1,0:T(8,128)(2,1)S(1)}, u32[]{:S(2)}, u32[]{:S(2)}) collective-permute-start(bf16[64,512]{1,0:T(8,128)(2,1)S(1)} %get-tuple-element.26), channel_id=1, source_target_pairs={{0,8},{4,12},{8,0},{12,4},{1,9},{5,13},{9,1},{13,5},{2,10},{6,14},... | collective-permute-start | bytes 196616 | tf_op jit(solution)/shard_map/ppermute | solution.py:41
  12.9 7.1 %collective-permute-start.5 = (bf16[2,64,512]{2,1,0:T(8,128)(2,1)S(1)}, bf16[2,64,512]{2,1,0:T(8,128)(2,1)S(1)}, u32[]{:S(2)}, u32[]{:S(2)}) collective-permute-start(bf16[2,64,512]{2,1,0:T(8,128)(2,1)S(1)} %pad_maximum_fusion.refs_0_), channel_id=1, source_target_pairs={{0,4},{4,0},{8,12},{12,8},{1,5},{5,1},{9,13},{13,9},{2,6},{6,2},{1... | collective-permute-start | bytes 393224 | tf_op jit(solution)/shard_map/ppermute | solution.py:41
  13.9 18.2 %collective-permute-start.4 = (bf16[1,32,1344]{2,1,0:T(8,128)(2,1)S(1)}, bf16[1,32,1344]{2,1,0:T(8,128)(2,1)S(1)}, u32[]{:S(2)}, u32[]{:S(2)}) collective-permute-start(bf16[1,32,1344]{2,1,0:T(8,128)(2,1)S(1)} %get-tuple-element.30._.refs_4_), channel_id=1, source_target_pairs={{0,2},{1,3},{2,0},{3,1},{4,6},{5,7},{6,4},{7,5},{8,10},{9,11},{10,... | collective-permute-start | bytes 258056 | tf_op jit(solution)/shard_map/ppermute | solution.py:41
  18.6 5.5 %collective-permute-start.11 = (bf16[2,64,512]{2,1,0:T(8,128)(2,1)S(1)}, bf16[2,64,512]{2,1,0:T(8,128)(2,1)S(1)}, u32[]{:S(2)}, u32[]{:S(2)}) collective-permute-start(bf16[2,64,512]{2,1,0:T(8,128)(2,1)S(1)} %stack.13.refs_1_), channel_id=1, source_target_pairs={{0,4},{4,0},{8,12},{12,8},{1,5},{5,1},{9,13},{13,9},{2,6},{6,2},{1... | collective-permute-start | bytes 393224 | tf_op jit(solution)/shard_map/ppermute | solution.py:41
  21.0 5.7 %collective-permute-start.8 = (bf16[2,32,1344]{2,1,0:T(8,128)(2,1)S(1)}, bf16[2,32,1344]{2,1,0:T(8,128)(2,1)S(1)}, u32[]{:S(2)}, u32[]{:S(2)}) collective-permute-start(bf16[2,32,1344]{2,1,0:T(8,128)(2,1)S(1)} %get-tuple-element.32.refs_3_), channel_id=1, source_target_pairs={{0,2},{1,3},{2,0},{3,1},{4,6},{5,7},{6,4},{7,5},{8,10},{9,11},{10,... | collective-permute-start | bytes 516104 | tf_op jit(solution)/shard_map/ppermute | solution.py:41
  25.0 11.5 %copy-start = (bf16[32,5376]{1,0:T(8,128)(2,1)S(1)}, bf16[32,5376]{1,0:T(8,128)(2,1)}, u32[]{:S(2)}) copy-start(bf16[32,5376]{1,0:T(8,128)(2,1)} %refs_5_.1) | copy-start | bytes 1032196
  25.0 4.9 %collective-permute-start.12 = (bf16[1,32,1344]{2,1,0:T(8,128)(2,1)S(1)}, bf16[1,32,1344]{2,1,0:T(8,128)(2,1)S(1)}, u32[]{:S(2)}, u32[]{:S(2)}) collective-permute-start(bf16[1,32,1344]{2,1,0:T(8,128)(2,1)S(1)} %get-tuple-element.34), channel_id=1, source_target_pairs={{0,2},{1,3},{2,0},{3,1},{4,6},{5,7},{6,4},{7,5},{8,10},{9,11},{10,... | collective-permute-start | bytes 258056 | tf_op jit(solution)/shard_map/ppermute | solution.py:41
  26.7 8.3 %collective-permute-start.10 = (bf16[32,1344]{1,0:T(8,128)(2,1)S(1)}, bf16[32,1344]{1,0:T(8,128)(2,1)S(1)}, u32[]{:S(2)}, u32[]{:S(2)}) collective-permute-start(bf16[32,1344]{1,0:T(8,128)(2,1)S(1)} %get-tuple-element.35._), channel_id=1, source_target_pairs={{0,8},{4,12},{8,0},{12,4},{1,9},{5,13},{9,1},{13,5},{2,10},{6,14},... | collective-permute-start | bytes 258056 | tf_op jit(solution)/shard_map/ppermute | solution.py:41
  29.5 5.5 %collective-permute-start.9 = (bf16[32,1344]{1,0:T(8,128)(2,1)S(1)}, bf16[32,1344]{1,0:T(8,128)(2,1)S(1)}, u32[]{:S(2)}, u32[]{:S(2)}) collective-permute-start(bf16[32,1344]{1,0:T(8,128)(2,1)S(1)} %finish.1), channel_id=1, source_target_pairs={{0,4},{4,0},{8,12},{12,8},{1,5},{5,1},{9,13},{13,9},{2,6},{6,2},{1... | collective-permute-start | bytes 258056 | tf_op jit(solution)/shard_map/ppermute | solution.py:41
  30.0 6.5 %collective-permute-start.13 = (bf16[32,1344]{1,0:T(8,128)(2,1)S(1)}, bf16[32,1344]{1,0:T(8,128)(2,1)S(1)}, u32[]{:S(2)}, u32[]{:S(2)}) collective-permute-start(bf16[32,1344]{1,0:T(8,128)(2,1)S(1)} %fusion.1), channel_id=1, source_target_pairs={{0,12},{4,8},{8,4},{12,0},{1,13},{5,9},{9,5},{13,1},{2,14},{6,10},... | collective-permute-start | bytes 258056 | tf_op jit(solution)/shard_map/ppermute | solution.py:41

commit v2 on v0

--- a/solution.py
+++ b/solution.py
@@ -339,9 +339,8 @@
 
 
 def norm(pieces, residual, post_gain):
-    early = None
-    for group in section_flips(len(pieces))[:-1]:
-        early = squares([pieces[flip] for flip in group], early)
+    last = last_flip(len(pieces))
+    early = squares([piece for flip, piece in enumerate(pieces) if flip != last], None)
     return pl.pallas_call(
         functools.partial(norm_kernel, len(pieces)),
         out_shape=jax.ShapeDtypeStruct(residual.shape, jnp.bfloat16),

time: 37.7 us -> 37.7 us (level)
  no operation moved by 1% of the time
where the time goes in v2:
time: 37.7 us; the launch traced here: 37.6 us
  starting transfers between devices  17.9 us (47%)
  waiting for transfers between devices  13.1 us (35%)
  Pallas kernels  6.28 us (17%)
    ppermute x11, starting transfers between devices, exchanged(): return lax.ppermute(value, axis, [(at, at ^ flip) for at in range(count)])  12.9 us
    ppermute x11, waiting for transfers between devices, exchanged(): return lax.ppermute(value, axis, [(at, at ^ flip) for at in range(count)])  10.3 us
    ppermute x2, starting transfers between devices, rotated(): lax.ppermute(value, axis, [(at, (at + steps) % count) for at in range(cou...  4.15 us
    pallas_call x3, Pallas kernels, project(): pl.pallas_call(functools.partial(project_kernel, [len(chunk) for chunk in...  2.89 us
    ppermute x2, waiting for transfers between devices, rotated(): lax.ppermute(value, axis, [(at, (at + steps) % count) for at in range(cou...  2.88 us
    pallas_call x1, Pallas kernels, attend(): pl.pallas_call(own_kernel, out_shape=(like(queries), like(values), like(t...  1.54 us
    pallas_call x1, Pallas kernels, norm(): pl.pallas_call(functools.partial(norm_kernel, len(pieces)), out_shape=jax...  1.12 us
    ppermute x1, starting transfers between devices, crossed(): return lax.ppermute(value, ('section', 'head'), pairs)  0.88 us
  transfers between devices with their start and end apart: 14, of which 8 were waited for; matrix products, arithmetic and copies ran while one was open for 0% of the time, Pallas kernels for 14%

profile of v2, /device:TPU:0, one launch (start us, length us, event | category | flops | bytes accessed | tf_op | source)
XLA Modules:
  0.0 37.6 jit_solution(14274291131525145304)
XLA Ops:
  0.0 0.5 %collective-permute-start.3 = (bf16[1344,512]{1,0:T(8,128)(2,1)}, bf16[1344,512]{1,0:T(8,128)(2,1)S(1)}, u32[]{:S(2)}, u32[]{:S(2)}) collective-permute-start(bf16[1344,512]{1,0:T(8,128)(2,1)} %bitcast.20), channel_id=1, source_target_pairs={{0,1},{1,0},{2,3},{3,2},{4,5},{5,4},{6,7},{7,6},{8,9},{9,8},{10,11... | collective-permute-start | bytes 4128776 | tf_op jit(solution)/shard_map/ppermute | solution.py:41
  0.5 2.6 %collective-permute-start = (bf16[1,128,256]{2,1,0:T(8,128)(2,1)}, bf16[1,128,256]{2,1,0:T(8,128)(2,1)S(1)}, u32[]{:S(2)}, u32[]{:S(2)}) collective-permute-start(bf16[1,128,256]{2,1,0:T(8,128)(2,1)} %bitcast.22), channel_id=1, source_target_pairs={{0,4},{4,8},{8,12},{12,0},{1,5},{5,9},{9,13},{13,1},{2,6},{6,10},{... | collective-permute-start | bytes 196616 | tf_op jit(solution)/shard_map/ppermute | solution.py:36
  3.0 0.0 copy-start.1
  3.0 1.6 %collective-permute-start.1 = (bf16[1,128,256]{2,1,0:T(8,128)(2,1)}, bf16[1,128,256]{2,1,0:T(8,128)(2,1)S(1)}, u32[]{:S(2)}, u32[]{:S(2)}) collective-permute-start(bf16[1,128,256]{2,1,0:T(8,128)(2,1)} %bitcast.23), channel_id=1, source_target_pairs={{0,4},{4,8},{8,12},{12,0},{1,5},{5,9},{9,13},{13,1},{2,6},{6,10},{... | collective-permute-start | bytes 196616 | tf_op jit(solution)/shard_map/ppermute | solution.py:36
  4.6 1.5 %own_scores.1 = (bf16[128,512]{1,0:T(8,128)(2,1)S(1)}, bf16[128,256]{1,0:T(8,128)(2,1)S(1)}, bf16[1344,512]{1,0:T(8,128)(2,1)S(1)}, f32[2,256,128]{2,1,0:T(8,128)S(1)}, f32[128,128]{1,0:T(8,128)S(1)}) custom-call(s32[4]{0:T(128)} %prefix_in.1, bf16[128,512]{1,0:T(8,128)(2,1)} %query_in.1, bf16[128,256]{1,0:T(8,128)(2,1)} %key_in.1, ...), custom_call_target="tpu_custom_call" | custom-call | tf_op jit(solution)/shard_map/own_scores/pallas_call | solution.py:175
  6.2 2.0 %collective-permute-done = bf16[1,128,256]{2,1,0:T(8,128)(2,1)S(1)} collective-permute-done((bf16[1,128,256]{2,1,0:T(8,128)(2,1)}, bf16[1,128,256]{2,1,0:T(8,128)(2,1)S(1)}, u32[]{:S(2)}, u32[]{:S(2)}) %collective-permute-start) | collective-permute-done | bytes 65568 | tf_op jit(solution)/shard_map/ppermute | solution.py:36
  8.2 0.4 %weigh.1 = (bf16[2,256,256]{2,1,0:T(8,128)(2,1)S(1)}, f32[2,256,128]{2,1,0:T(8,128)S(1)}) custom-call(bf16[128,512]{1,0:T(8,128)(2,1)S(1)} %get-tuple-element.20.query_ref, f32[2,256,128]{2,1,0:T(8,128)S(1)} %get-tuple-element.21.score_ref, f32[128,128]{1,0:T(8,128)S(1)} %get-tuple-element.22.bias_ref, bf16[128,256]{1,0:T(8,128)(2,1)S(1)} %bitcast.19), custom_call_target="tpu_custom_call" | custom-call | tf_op jit(solution)/shard_map/weigh/pallas_call | solution.py:196
  8.6 0.8 %collective-permute-done.1 = bf16[1,128,256]{2,1,0:T(8,128)(2,1)S(1)} collective-permute-done((bf16[1,128,256]{2,1,0:T(8,128)(2,1)}, bf16[1,128,256]{2,1,0:T(8,128)(2,1)S(1)}, u32[]{:S(2)}, u32[]{:S(2)}) %collective-permute-start.1) | collective-permute-done | bytes 65568 | tf_op jit(solution)/shard_map/ppermute | solution.py:36
  9.4 0.2 attend.1
  9.7 0.1 collective-permute-start.2
  9.7 0.0 copy-done.1
  9.8 0.9 %collective-permute-start.7 = (bf16[64,512]{1,0:T(8,128)(2,1)S(1)}, bf16[64,512]{1,0:T(8,128)(2,1)S(1)}, u32[]{:S(2)}, u32[]{:S(2)}) collective-permute-start(bf16[64,512]{1,0:T(8,128)(2,1)S(1)} %get-tuple-element.27), channel_id=1, source_target_pairs={{0,9},{1,8},{2,11},{3,10},{4,13},{5,12},{6,15},{7,14},{8,1},{9,0},... | collective-permute-start | bytes 196616 | tf_op jit(solution)/shard_map/ppermute | solution.py:51
  10.7 2.2 %collective-permute-start.6 = (bf16[64,512]{1,0:T(8,128)(2,1)S(1)}, bf16[64,512]{1,0:T(8,128)(2,1)S(1)}, u32[]{:S(2)}, u32[]{:S(2)}) collective-permute-start(bf16[64,512]{1,0:T(8,128)(2,1)S(1)} %get-tuple-element.26), channel_id=1, source_target_pairs={{0,8},{4,12},{8,0},{12,4},{1,9},{5,13},{9,1},{13,5},{2,10},{6,14},... | collective-permute-start | bytes 196616 | tf_op jit(solution)/shard_map/ppermute | solution.py:41
  12.8 0.0 collective-permute-done.2
  12.9 0.1 collective-permute-start.5
  12.9 0.0 collective-permute-done.3.refs_2_.refs_3_
  13.0 0.9 %project.3 = (bf16[1,32,1344]{2,1,0:T(8,128)(2,1)S(1)}, f32[1,32,1344]{2,1,0:T(8,128)S(1)}) custom-call(bf16[2,64,512]{2,1,0:T(8,128)(2,1)S(1)} %pad_maximum_fusion.refs_0_, bf16[1344,512]{1,0:T(8,128)(2,1)S(1)} %get-tuple-element.28.refs_1_.refs_2_, bf16[1344,512]{1,0:T(8,128)(2,1)S(1)} %collective-permute-done.3.refs_2_.refs_3_), custom_call_target="tpu_custom_call" | custom-call | flops 3000000000 | tf_op jit(solution)/shard_map/project/pallas_call | solution.py:248
  13.9 1.6 %collective-permute-start.4 = (bf16[1,32,1344]{2,1,0:T(8,128)(2,1)S(1)}, bf16[1,32,1344]{2,1,0:T(8,128)(2,1)S(1)}, u32[]{:S(2)}, u32[]{:S(2)}) collective-permute-start(bf16[1,32,1344]{2,1,0:T(8,128)(2,1)S(1)} %get-tuple-element.30._.refs_4_), channel_id=1, source_target_pairs={{0,2},{1,3},{2,0},{3,1},{4,6},{5,7},{6,4},{7,5},{8,10},{9,11},{10,... | collective-permute-start | bytes 258056 | tf_op jit(solution)/shard_map/ppermute | solution.py:41
  15.5 3.1 %collective-permute-done.6.own_ref = bf16[64,512]{1,0:T(8,128)(2,1)S(1)} collective-permute-done((bf16[64,512]{1,0:T(8,128)(2,1)S(1)}, bf16[64,512]{1,0:T(8,128)(2,1)S(1)}, u32[]{:S(2)}, u32[]{:S(2)}) %collective-permute-start.6) | collective-permute-done | bytes 65568 | tf_op jit(solution)/shard_map/ppermute | solution.py:41
  18.6 0.0 collective-permute-done.7.other_ref
  18.6 0.1 collective-permute-start.11
  18.7 1.3 %collective-permute-done.5.refs_0_ = bf16[2,64,512]{2,1,0:T(8,128)(2,1)S(1)} collective-permute-done((bf16[2,64,512]{2,1,0:T(8,128)(2,1)S(1)}, bf16[2,64,512]{2,1,0:T(8,128)(2,1)S(1)}, u32[]{:S(2)}, u32[]{:S(2)}) %collective-permute-start.5) | collective-permute-done | bytes 131104 | tf_op jit(solution)/shard_map/ppermute | solution.py:41
  19.9 1.0 %project.4 = (bf16[2,32,1344]{2,1,0:T(8,128)(2,1)S(1)}, f32[2,32,1344]{2,1,0:T(8,128)S(1)}) custom-call(bf16[2,64,512]{2,1,0:T(8,128)(2,1)S(1)} %collective-permute-done.5.refs_0_, bf16[2,64,512]{2,1,0:T(8,128)(2,1)S(1)} %stack.13.refs_1_, bf16[1344,512]{1,0:T(8,128)(2,1)S(1)} %get-tuple-element.28.refs_1_.refs_2_, ...), custom_call_target="tpu_custom_call" | custom-call | flops 3000000000 | tf_op jit(solution)/shard_map/project/pallas_call | solution.py:248
  21.0 1.6 %collective-permute-start.8 = (bf16[2,32,1344]{2,1,0:T(8,128)(2,1)S(1)}, bf16[2,32,1344]{2,1,0:T(8,128)(2,1)S(1)}, u32[]{:S(2)}, u32[]{:S(2)}) collective-permute-start(bf16[2,32,1344]{2,1,0:T(8,128)(2,1)S(1)} %get-tuple-element.32.refs_3_), channel_id=1, source_target_pairs={{0,2},{1,3},{2,0},{3,1},{4,6},{5,7},{6,4},{7,5},{8,10},{9,11},{10,... | collective-permute-start | bytes 516104 | tf_op jit(solution)/shard_map/ppermute | solution.py:41
  22.5 1.5 %collective-permute-done.11.refs_0_ = bf16[2,64,512]{2,1,0:T(8,128)(2,1)S(1)} collective-permute-done((bf16[2,64,512]{2,1,0:T(8,128)(2,1)S(1)}, bf16[2,64,512]{2,1,0:T(8,128)(2,1)S(1)}, u32[]{:S(2)}, u32[]{:S(2)}) %collective-permute-start.11) | collective-permute-done | bytes 131104 | tf_op jit(solution)/shard_map/ppermute | solution.py:41
  24.1 0.9 %project.5 = (bf16[1,32,1344]{2,1,0:T(8,128)(2,1)S(1)}, f32[1,32,1344]{2,1,0:T(8,128)S(1)}) custom-call(bf16[2,64,512]{2,1,0:T(8,128)(2,1)S(1)} %collective-permute-done.11.refs_0_, bf16[1344,512]{1,0:T(8,128)(2,1)S(1)} %get-tuple-element.28.refs_1_.refs_2_, bf16[1344,512]{1,0:T(8,128)(2,1)S(1)} %collective-permute-done.3.refs_2_.refs_3_, ...), custom_call_target="tpu_custom_call" | custom-call | flops 3000000000 | tf_op jit(solution)/shard_map/project/pallas_call | solution.py:248
  25.0 0.0 copy-start
  25.0 1.6 %collective-permute-start.12 = (bf16[1,32,1344]{2,1,0:T(8,128)(2,1)S(1)}, bf16[1,32,1344]{2,1,0:T(8,128)(2,1)S(1)}, u32[]{:S(2)}, u32[]{:S(2)}) collective-permute-start(bf16[1,32,1344]{2,1,0:T(8,128)(2,1)S(1)} %get-tuple-element.34), channel_id=1, source_target_pairs={{0,2},{1,3},{2,0},{3,1},{4,6},{5,7},{6,4},{7,5},{8,10},{9,11},{10,... | collective-permute-start | bytes 258056 | tf_op jit(solution)/shard_map/ppermute | solution.py:41
  26.6 0.1 collective-permute-done.8
  26.7 2.8 %collective-permute-start.10 = (bf16[32,1344]{1,0:T(8,128)(2,1)S(1)}, bf16[32,1344]{1,0:T(8,128)(2,1)S(1)}, u32[]{:S(2)}, u32[]{:S(2)}) collective-permute-start(bf16[32,1344]{1,0:T(8,128)(2,1)S(1)} %get-tuple-element.35._), channel_id=1, source_target_pairs={{0,8},{4,12},{8,0},{12,4},{1,9},{5,13},{9,1},{13,5},{2,10},{6,14},... | collective-permute-start | bytes 258056 | tf_op jit(solution)/shard_map/ppermute | solution.py:41
  29.5 0.4 %collective-permute-start.9 = (bf16[32,1344]{1,0:T(8,128)(2,1)S(1)}, bf16[32,1344]{1,0:T(8,128)(2,1)S(1)}, u32[]{:S(2)}, u32[]{:S(2)}) collective-permute-start(bf16[32,1344]{1,0:T(8,128)(2,1)S(1)} %finish.1), channel_id=1, source_target_pairs={{0,4},{4,0},{8,12},{12,8},{1,5},{5,1},{9,13},{13,9},{2,6},{6,2},{1... | collective-permute-start | bytes 258056 | tf_op jit(solution)/shard_map/ppermute | solution.py:41
  30.0 0.0 collective-permute-done.12
  30.0 2.2 %collective-permute-start.13 = (bf16[32,1344]{1,0:T(8,128)(2,1)S(1)}, bf16[32,1344]{1,0:T(8,128)(2,1)S(1)}, u32[]{:S(2)}, u32[]{:S(2)}) collective-permute-start(bf16[32,1344]{1,0:T(8,128)(2,1)S(1)} %fusion.1), channel_id=1, source_target_pairs={{0,12},{4,8},{8,4},{12,0},{1,13},{5,9},{9,5},{13,1},{2,14},{6,10},... | collective-permute-start | bytes 258056 | tf_op jit(solution)/shard_map/ppermute | solution.py:41
  32.1 0.0 collective-permute-done.4
  32.2 2.9 %collective-permute-done.9.refs_1_ = bf16[32,1344]{1,0:T(8,128)(2,1)S(1)} collective-permute-done((bf16[32,1344]{1,0:T(8,128)(2,1)S(1)}, bf16[32,1344]{1,0:T(8,128)(2,1)S(1)}, u32[]{:S(2)}, u32[]{:S(2)}) %collective-permute-start.9) | collective-permute-done | bytes 86048 | tf_op jit(solution)/shard_map/ppermute | solution.py:41
  35.0 0.0 collective-permute-done.10.refs_2_
  35.0 0.1 squares.1.refs_4_
  35.2 1.3 %collective-permute-done.13.refs_3_ = bf16[32,1344]{1,0:T(8,128)(2,1)S(1)} collective-permute-done((bf16[32,1344]{1,0:T(8,128)(2,1)S(1)}, bf16[32,1344]{1,0:T(8,128)(2,1)S(1)}, u32[]{:S(2)}, u32[]{:S(2)}) %collective-permute-start.13) | collective-permute-done | bytes 86048 | tf_op jit(solution)/shard_map/ppermute | solution.py:41
  36.5 0.0 copy-done
  36.5 1.1 %norm.1 = bf16[32,5376]{1,0:T(8,128)(2,1)} custom-call(f32[32,1344]{1,0:T(8,128)S(1)} %add_bitcast_fusion.refs_0_, bf16[32,1344]{1,0:T(8,128)(2,1)S(1)} %collective-permute-done.9.refs_1_, bf16[32,1344]{1,0:T(8,128)(2,1)S(1)} %collective-permute-done.10.refs_2_, bf16[32,1344]{1,0:T(8,128)(2,1)S(1)} %collective-permute-done.13.refs_3_, ...), custom_call_target="tpu_custom_call" | custom-call | tf_op jit(solution)/shard_map/norm/pallas_call | solution.py:344
  (8 shorter events, 0.1 us)
Async XLA Ops:
  0.0 13.0 %collective-permute-start.3 = (bf16[1344,512]{1,0:T(8,128)(2,1)}, bf16[1344,512]{1,0:T(8,128)(2,1)S(1)}, u32[]{:S(2)}, u32[]{:S(2)}) collective-permute-start(bf16[1344,512]{1,0:T(8,128)(2,1)} %bitcast.20), channel_id=1, source_target_pairs={{0,1},{1,0},{2,3},{3,2},{4,5},{5,4},{6,7},{7,6},{8,9},{9,8},{10,11... | collective-permute-start | bytes 4128776 | tf_op jit(solution)/shard_map/ppermute | solution.py:41
  0.5 7.7 %collective-permute-start = (bf16[1,128,256]{2,1,0:T(8,128)(2,1)}, bf16[1,128,256]{2,1,0:T(8,128)(2,1)S(1)}, u32[]{:S(2)}, u32[]{:S(2)}) collective-permute-start(bf16[1,128,256]{2,1,0:T(8,128)(2,1)} %bitcast.22), channel_id=1, source_target_pairs={{0,4},{4,8},{8,12},{12,0},{1,5},{5,9},{9,13},{13,1},{2,6},{6,10},{... | collective-permute-start | bytes 196616 | tf_op jit(solution)/shard_map/ppermute | solution.py:36
  3.0 6.7 %copy-start.1 = (f32[5376]{0:T(1024)S(1)}, f32[5376]{0:T(1024)}, u32[]{:S(2)}) copy-start(f32[5376]{0:T(1024)} %param.13) | copy-start | bytes 64516
  3.0 6.4 %collective-permute-start.1 = (bf16[1,128,256]{2,1,0:T(8,128)(2,1)}, bf16[1,128,256]{2,1,0:T(8,128)(2,1)S(1)}, u32[]{:S(2)}, u32[]{:S(2)}) collective-permute-start(bf16[1,128,256]{2,1,0:T(8,128)(2,1)} %bitcast.23), channel_id=1, source_target_pairs={{0,4},{4,8},{8,12},{12,0},{1,5},{5,9},{9,13},{13,1},{2,6},{6,10},{... | collective-permute-start | bytes 196616 | tf_op jit(solution)/shard_map/ppermute | solution.py:36
  9.7 3.2 %collective-permute-start.2 = (bf16[64,512]{1,0:T(8,128)(2,1)S(1)}, bf16[64,512]{1,0:T(8,128)(2,1)S(1)}, u32[]{:S(2)}, u32[]{:S(2)}) collective-permute-start(bf16[64,512]{1,0:T(8,128)(2,1)S(1)} %get-tuple-element.27), channel_id=1, source_target_pairs={{0,1},{1,0},{2,3},{3,2},{4,5},{5,4},{6,7},{7,6},{8,9},{9,8},{10,11... | collective-permute-start | bytes 196616 | tf_op jit(solution)/shard_map/ppermute | solution.py:41
  9.8 8.8 %collective-permute-start.7 = (bf16[64,512]{1,0:T(8,128)(2,1)S(1)}, bf16[64,512]{1,0:T(8,128)(2,1)S(1)}, u32[]{:S(2)}, u32[]{:S(2)}) collective-permute-start(bf16[64,512]{1,0:T(8,128)(2,1)S(1)} %get-tuple-element.27), channel_id=1, source_target_pairs={{0,9},{1,8},{2,11},{3,10},{4,13},{5,12},{6,15},{7,14},{8,1},{9,0},... | collective-permute-start | bytes 196616 | tf_op jit(solution)/shard_map/ppermute | solution.py:51
  10.7 7.9 %collective-permute-start.6 = (bf16[64,512]{1,0:T(8,128)(2,1)S(1)}, bf16[64,512]{1,0:T(8,128)(2,1)S(1)}, u32[]{:S(2)}, u32[]{:S(2)}) collective-permute-start(bf16[64,512]{1,0:T(8,128)(2,1)S(1)} %get-tuple-element.26), channel_id=1, source_target_pairs={{0,8},{4,12},{8,0},{12,4},{1,9},{5,13},{9,1},{13,5},{2,10},{6,14},... | collective-permute-start | bytes 196616 | tf_op jit(solution)/shard_map/ppermute | solution.py:41
  12.9 7.1 %collective-permute-start.5 = (bf16[2,64,512]{2,1,0:T(8,128)(2,1)S(1)}, bf16[2,64,512]{2,1,0:T(8,128)(2,1)S(1)}, u32[]{:S(2)}, u32[]{:S(2)}) collective-permute-start(bf16[2,64,512]{2,1,0:T(8,128)(2,1)S(1)} %pad_maximum_fusion.refs_0_), channel_id=1, source_target_pairs={{0,4},{4,0},{8,12},{12,8},{1,5},{5,1},{9,13},{13,9},{2,6},{6,2},{1... | collective-permute-start | bytes 393224 | tf_op jit(solution)/shard_map/ppermute | solution.py:41
  13.9 18.2 %collective-permute-start.4 = (bf16[1,32,1344]{2,1,0:T(8,128)(2,1)S(1)}, bf16[1,32,1344]{2,1,0:T(8,128)(2,1)S(1)}, u32[]{:S(2)}, u32[]{:S(2)}) collective-permute-start(bf16[1,32,1344]{2,1,0:T(8,128)(2,1)S(1)} %get-tuple-element.30._.refs_4_), channel_id=1, source_target_pairs={{0,2},{1,3},{2,0},{3,1},{4,6},{5,7},{6,4},{7,5},{8,10},{9,11},{10,... | collective-permute-start | bytes 258056 | tf_op jit(solution)/shard_map/ppermute | solution.py:41
  18.6 5.5 %collective-permute-start.11 = (bf16[2,64,512]{2,1,0:T(8,128)(2,1)S(1)}, bf16[2,64,512]{2,1,0:T(8,128)(2,1)S(1)}, u32[]{:S(2)}, u32[]{:S(2)}) collective-permute-start(bf16[2,64,512]{2,1,0:T(8,128)(2,1)S(1)} %stack.13.refs_1_), channel_id=1, source_target_pairs={{0,4},{4,0},{8,12},{12,8},{1,5},{5,1},{9,13},{13,9},{2,6},{6,2},{1... | collective-permute-start | bytes 393224 | tf_op jit(solution)/shard_map/ppermute | solution.py:41
  21.0 5.7 %collective-permute-start.8 = (bf16[2,32,1344]{2,1,0:T(8,128)(2,1)S(1)}, bf16[2,32,1344]{2,1,0:T(8,128)(2,1)S(1)}, u32[]{:S(2)}, u32[]{:S(2)}) collective-permute-start(bf16[2,32,1344]{2,1,0:T(8,128)(2,1)S(1)} %get-tuple-element.32.refs_3_), channel_id=1, source_target_pairs={{0,2},{1,3},{2,0},{3,1},{4,6},{5,7},{6,4},{7,5},{8,10},{9,11},{10,... | collective-permute-start | bytes 516104 | tf_op jit(solution)/shard_map/ppermute | solution.py:41
  25.0 11.5 %copy-start = (bf16[32,5376]{1,0:T(8,128)(2,1)S(1)}, bf16[32,5376]{1,0:T(8,128)(2,1)}, u32[]{:S(2)}) copy-start(bf16[32,5376]{1,0:T(8,128)(2,1)} %refs_5_.1) | copy-start | bytes 1032196
  25.0 4.9 %collective-permute-start.12 = (bf16[1,32,1344]{2,1,0:T(8,128)(2,1)S(1)}, bf16[1,32,1344]{2,1,0:T(8,128)(2,1)S(1)}, u32[]{:S(2)}, u32[]{:S(2)}) collective-permute-start(bf16[1,32,1344]{2,1,0:T(8,128)(2,1)S(1)} %get-tuple-element.34), channel_id=1, source_target_pairs={{0,2},{1,3},{2,0},{3,1},{4,6},{5,7},{6,4},{7,5},{8,10},{9,11},{10,... | collective-permute-start | bytes 258056 | tf_op jit(solution)/shard_map/ppermute | solution.py:41
  26.7 8.3 %collective-permute-start.10 = (bf16[32,1344]{1,0:T(8,128)(2,1)S(1)}, bf16[32,1344]{1,0:T(8,128)(2,1)S(1)}, u32[]{:S(2)}, u32[]{:S(2)}) collective-permute-start(bf16[32,1344]{1,0:T(8,128)(2,1)S(1)} %get-tuple-element.35._), channel_id=1, source_target_pairs={{0,8},{4,12},{8,0},{12,4},{1,9},{5,13},{9,1},{13,5},{2,10},{6,14},... | collective-permute-start | bytes 258056 | tf_op jit(solution)/shard_map/ppermute | solution.py:41
  29.5 5.5 %collective-permute-start.9 = (bf16[32,1344]{1,0:T(8,128)(2,1)S(1)}, bf16[32,1344]{1,0:T(8,128)(2,1)S(1)}, u32[]{:S(2)}, u32[]{:S(2)}) collective-permute-start(bf16[32,1344]{1,0:T(8,128)(2,1)S(1)} %finish.1), channel_id=1, source_target_pairs={{0,4},{4,0},{8,12},{12,8},{1,5},{5,1},{9,13},{13,9},{2,6},{6,2},{1... | collective-permute-start | bytes 258056 | tf_op jit(solution)/shard_map/ppermute | solution.py:41
  30.0 6.5 %collective-permute-start.13 = (bf16[32,1344]{1,0:T(8,128)(2,1)S(1)}, bf16[32,1344]{1,0:T(8,128)(2,1)S(1)}, u32[]{:S(2)}, u32[]{:S(2)}) collective-permute-start(bf16[32,1344]{1,0:T(8,128)(2,1)S(1)} %fusion.1), channel_id=1, source_target_pairs={{0,12},{4,8},{8,4},{12,0},{1,13},{5,9},{9,5},{13,1},{2,14},{6,10},... | collective-permute-start | bytes 258056 | tf_op jit(solution)/shard_map/ppermute | solution.py:41
